TPU v7x, 32 devices: a whole 2x2x4 slice. The times are simulated.
32 devices in a mesh: case: 2 (over x), span: 8 (over z, y), dom: 2 (over core).
Axes of the slice: x: 2, y: 2, z: 4, core: 2. Of those that a mesh axis runs over, the one named last changes fastest.
Arguments:
- scalar: float32 [256, 8192], P(('case', 'span'), 'dom'), parts along dimension 0, may hold values from -6 to 6
- span_vel: float32 [256, 8192], P(('case', 'span'), 'dom'), parts along dimension 0, may hold values from -4 to 4
- flux_weight: float32 [4, 8192], P(None, 'dom'), may hold values from -4 to 4
- neighbours: int32 [4, 8192], P(None, 'dom'), may hold values from 0 to 8191, as said below
- diagonal: float32 [8192], P('dom'), may hold values from 0.5 to 2
- interface: int32 [16, 128], P('dom'), may hold values from 0 to 8191, as said below
- schur_one: float32 [128, 8, 128, 128], P('span', 'dom'), may hold values from -1 to 1
- schur_two: float32 [128, 4, 128, 128], P('span', 'dom'), may hold values from -1 to 1
- schur_three: float32 [128, 2, 128, 128], P('span', 'dom'), may hold values from -1 to 1
- schur_root: float32 [128, 1, 128, 128], P('span'), may hold values from -1 to 1
Outputs:
- pressure: float32 [256, 8192], P(('case', 'span'), 'dom'), parts along dimension 0
- corrected: float32 [256, 8192], P(('case', 'span'), 'dom'), parts along dimension 0
There are 2 independent parts, one for each index of `case`. A program takes and returns all parts, laid end to end along the dimension named above; an argument that names none is the same for every part. Nothing has to cross between parts.
Inputs may be any that keep to these rules, and one draw needn't show every extreme that they name: `neighbours`: every entry lies 1 to 64 cells from its own cell in the numbering, and the distance 64 occurs. `interface`: row d holds 128 distinct cells of subdomain d, numbered from d * 512 to (d + 1) * 512 - 1.
All inputs are finite; a program needn't handle non-finite values.
Results may differ from a plain program's by a relative error of at most 0.0001.
Values sent between devices are 32-bit elements; how exact they have to be, the bound alone decides.
A program may use at most 64 MiB of HBM per device.

v0:
```python
import math

import jax
import jax.numpy as jnp
from jax import lax
from jax.sharding import PartitionSpec as P

PLANES = 128
CELL_DOM = 512
HALO = 64


def extended(value, sides, width, wrap):
    for axis, dim in sides:
        count, length = (lax.axis_size(axis), value.shape[dim])
        up = [(i, (i + 1) % count) for i in range(count if wrap else count - 1)]
        down = [(j, i) for i, j in up]
        last = lax.slice_in_dim(value, length - width, length, axis=dim)
        initial = lax.slice_in_dim(value, 0, width, axis=dim)
        before = lax.ppermute(last, axis, up)
        after = lax.ppermute(initial, axis, down)
        value = jnp.concatenate([before, value, after], axis=dim)
    return value


def swapped(value, axis, distance):
    return lax.ppermute(value, axis, [(i, i ^ 1 << distance) for i in range(lax.axis_size(axis))])


def fourier_entry(wave_ids, plane_ids):
    middle = PLANES // 2
    wave_num = jnp.where(wave_ids <= middle, wave_ids, wave_ids - middle)
    phase_angle = (wave_num * plane_ids % PLANES).astype(jnp.float32) * (2.0 * math.pi / PLANES)
    at_edge = (wave_ids == 0) | (wave_ids == middle)
    weight_row = jnp.where(at_edge, math.sqrt(1.0 / PLANES), math.sqrt(2.0 / PLANES))
    return jnp.where(wave_ids <= middle, jnp.cos(phase_angle), jnp.sin(phase_angle)) * weight_row


def wave_shift(wave_ids):
    middle = PLANES // 2
    wave_num = jnp.where(wave_ids <= middle, wave_ids, wave_ids - middle).astype(jnp.float32)
    return (2.0 * jnp.sin(wave_num * (math.pi / PLANES))) ** 2


def stencil(field, span_vel, flux_weight, near_local):
    planes_ext = extended(field, (("span", 0),), 1, True)
    convected = span_vel * 0.5 * (planes_ext[2:] - planes_ext[:-2])
    widened = extended(field, (("dom", 1),), HALO, False)
    for slot in range(flux_weight.shape[0]):
        convected = convected + flux_weight[slot] * (widened[:, near_local[slot]] - field)
    return convected


def apply_table(table, block):
    return jnp.einsum("rp,pxc->rxc", table, block, precision=lax.Precision.HIGHEST)


def on_device(
    scalar,
    span_vel,
    flux_weight,
    neighbours,
    diagonal,
    interface,
    schur_one,
    schur_two,
    schur_three,
    schur_root,
):
    plane_count = scalar.shape[0]
    cell_count = scalar.shape[1]
    span_count = lax.axis_size("span")
    span_pos = lax.axis_index("span")
    cols_count = cell_count // span_count
    cell_start = lax.axis_index("dom") * cell_count
    near_local = neighbours - cell_start + HALO
    source = scalar - stencil(scalar, span_vel, flux_weight, near_local)
    all_waves = jnp.arange(PLANES, dtype=jnp.int32)
    local_iface = interface - cell_start
    wave_table = fourier_entry(all_waves[:, None], all_waves[None, :])
    slot_count = min(cols_count, interface.shape[1] * max(1, cols_count // CELL_DOM))
    grouped = source.reshape(plane_count, span_count, cols_count)
    spectrum_cols = apply_table(
        wave_table, lax.all_to_all(grouped, "span", split_axis=1, concat_axis=0, tiled=True)
    ).reshape(PLANES, cols_count)
    diag_cols = lax.dynamic_slice_in_dim(diagonal, span_pos * cols_count, cols_count)
    interior_cols = spectrum_cols / (diag_cols[None, :] + wave_shift(all_waves)[:, None])
    flat_iface = local_iface.reshape(-1)
    owner = flat_iface // cols_count
    onehot = (owner[:, None] == jnp.arange(span_count, dtype=jnp.int32)[None, :]).astype(jnp.int32)
    ranks = jnp.sum(jnp.cumsum(onehot, 0) * onehot, 1) - 1
    slot_index = owner * slot_count + ranks
    owned = owner == span_pos
    slot_cell = (
        jnp.full((slot_count,), cols_count, jnp.int32)
        .at[jnp.where(owned, ranks, slot_count)]
        .set(flat_iface - span_pos * cols_count, mode="drop")
    )
    payload = interior_cols[:, jnp.minimum(slot_cell, cols_count - 1)]
    received = lax.all_to_all(payload, "span", split_axis=0, concat_axis=1, tiled=True)
    leaves = received[:, slot_index].reshape(
        plane_count, local_iface.shape[0], local_iface.shape[1]
    )
    levels = [leaves]
    current = leaves
    for blocks in (schur_one, schur_two, schur_three):
        paired = current[:, 0::2] + current[:, 1::2]
        current = jnp.einsum("mnij,mnj->mni", blocks, paired, precision=lax.Precision.HIGHEST)
        levels.append(current)
    partner = swapped(current, "dom", 0)
    top_value = jnp.einsum(
        "mnij,mnj->mni", schur_root, current + partner, precision=lax.Precision.HIGHEST
    )
    returned = jnp.einsum("mnji,mnj->mni", schur_root, top_value, precision=lax.Precision.HIGHEST)
    lowered = levels[3] - returned
    for blocks, below in ((schur_three, levels[2]), (schur_two, levels[1]), (schur_one, levels[0])):
        returned = jnp.einsum("mnji,mnj->mni", blocks, lowered, precision=lax.Precision.HIGHEST)
        lowered = below - jnp.repeat(returned, 2, axis=1)
    outgoing = (
        jnp.zeros((plane_count, span_count * slot_count), jnp.float32)
        .at[:, slot_index]
        .set(0.5 * lowered.reshape(plane_count, -1))
    )
    back_slots = lax.all_to_all(outgoing, "span", split_axis=1, concat_axis=0, tiled=True)
    corrected_cols = interior_cols.at[:, slot_cell].add(-back_slots, mode="drop")
    pressure_cols = jnp.dot(wave_table.T, corrected_cols, precision=lax.Precision.HIGHEST)
    pressure = lax.all_to_all(pressure_cols, "span", split_axis=0, concat_axis=1, tiled=True)
    corrected = scalar - stencil(pressure, span_vel, flux_weight, near_local)
    return (pressure, corrected)


def solution(mesh):
    placed = (
        P(("case", "span"), "dom"),
        P(("case", "span"), "dom"),
        P(None, "dom"),
        P(None, "dom"),
        P("dom"),
        P("dom", None),
        P("span", "dom", None, None),
        P("span", "dom", None, None),
        P("span", "dom", None, None),
        P("span", None, None, None),
    )
    return jax.shard_map(
        on_device,
        mesh=mesh,
        in_specs=placed,
        out_specs=(P(("case", "span"), "dom"), P(("case", "span"), "dom")),
        check_vma=False,
    )
```

profile of v0, /device:TPU:0, one launch (start us, length us, event | category | flops | bytes accessed | tf_op | source)
XLA Modules:
  0.0 271.5 jit_solution(5067358986018069277)
XLA Ops:
  2.9 3.0 %collective-permute-start.2 = (f32[16,64]{1,0:T(8,128)S(1)}, f32[16,64]{1,0:T(8,128)S(1)}, u32[]{:S(2)}, u32[]{:S(2)}) collective-permute-start(f32[16,64]{1,0:T(8,128)S(1)} %get-tuple-element.19), channel_id=1, source_target_pairs={{0,1},{2,3},{4,5},{6,7},{8,9},{10,11},{12,13},{14,15},{16,17},{18,... | collective-permute-start | bytes 12296 | tf_op jit(solution)/shard_map/ppermute | solution.py:20
  7.5 6.0 %collective-permute-start = (f32[1,4096]{1,0:T(1,128)}, f32[1,4096]{1,0:T(1,128)S(1)}, u32[]{:S(2)}, u32[]{:S(2)}) collective-permute-start(f32[1,4096]{1,0:T(1,128)} %get-tuple-element.20), channel_id=1, source_target_pairs={{2,0},{4,2},{6,4},{8,6},{10,8},{12,10},{14,12},{0,14},{3,1},{5,3},... | collective-permute-start | bytes 49160 | tf_op jit(solution)/shard_map/ppermute | solution.py:21
  14.8 2.3 reduce-window.6
  24.7 15.7 %gather_fusion.3 = f32[4096,16]{1,0:T(8,128)} fusion(f32[16,4224]{0,1:T(8,128)} %copy.121, s32[4096]{0:T(1024)S(1)} %broadcast_clamp_fusion), kind=kCustom, calls=%fused_computation.3 | custom fusion | bytes 540672 | tf_op jit(solution)/shard_map/gather | solution.py:50
  40.4 2.2 copy.128
  42.6 15.7 %gather_fusion.2 = f32[4096,16]{1,0:T(8,128)} fusion(f32[16,4224]{0,1:T(8,128)} %copy.121, s32[4096]{0:T(1024)S(1)} %broadcast_clamp_fusion.1), kind=kCustom, calls=%fused_computation.2 | custom fusion | bytes 540672 | tf_op jit(solution)/shard_map/gather | solution.py:50
  58.3 2.2 copy.126
  60.4 15.7 %gather_fusion.1 = f32[4096,16]{1,0:T(8,128)} fusion(f32[16,4224]{0,1:T(8,128)} %copy.121, s32[4096]{0:T(1024)S(1)} %broadcast_clamp_fusion.2), kind=kCustom, calls=%fused_computation.1 | custom fusion | bytes 540672 | tf_op jit(solution)/shard_map/gather | solution.py:50
  76.2 2.2 copy.124
  78.3 15.8 %gather_fusion = f32[4096,16]{1,0:T(8,128)} fusion(f32[16,4224]{0,1:T(8,128)} %copy.121, s32[4096]{0:T(1024)S(1)} %broadcast_clamp_fusion.3), kind=kCustom, calls=%fused_computation | custom fusion | bytes 540672 | tf_op jit(solution)/shard_map/gather | solution.py:50
  94.1 2.9 %copy.122 = f32[4096,16]{0,1:T(8,128)} copy(f32[4096,16]{1,0:T(8,128)} %gather_fusion) | data formatting | bytes 524288 | tf_op jit(solution)/shard_map/gather | solution.py:50
  98.9 6.0 %all-to-all-start = ((f32[16,8,512]{2,0,1:T(8,128)}), f32[16,8,512]{2,0,1:T(8,128)S(1)}, u32[]{:S(2)}, u32[]{:S(2)}) async-start(f32[16,8,512]{2,0,1:T(8,128)} %bitcast.210), calls=%async_computation | async-start | bytes 524288 | tf_op jit(solution)/shard_map/all_to_all | solution.py:84
  105.7 4.4 %scatter_custom_fusion = s32[128]{0:T(128)S(1)} fusion(s32[1024]{0:T(1024)} %bitcast.265, s32[1024]{0:T(1024)} %get-tuple-element.12, s32[]{:T(128)} %constant.72.clone.1), kind=kCustom, calls=%fused_computation.133 | custom fusion | bytes 1024 | tf_op jit(solution)/shard_map/scatter | solution.py:97
  110.7 2.4 all-to-all-done
  116.0 3.6 %all-to-all-start.1 = ((f32[8,16,128]{2,1,0:T(8,128)}), f32[8,16,128]{2,1,0:T(8,128)S(1)}, u32[]{:S(2)}, u32[]{:S(2)}) async-start(f32[8,16,128]{2,1,0:T(8,128)} %bitcast.26), calls=%async_computation.1 | async-start | bytes 131072 | tf_op jit(solution)/shard_map/all_to_all | solution.py:100
  119.6 6.9 %all-to-all-done.1 = f32[8,16,128]{2,1,0:T(8,128)S(1)} async-done(((f32[8,16,128]{2,1,0:T(8,128)}), f32[8,16,128]{2,1,0:T(8,128)S(1)}, u32[]{:S(2)}, u32[]{:S(2)}) %all-to-all-start.1) | async-done | bytes 65568 | tf_op jit(solution)/shard_map/all_to_all | solution.py:100
  126.7 2.8 %gather_fusion.5 = f32[1024,16]{1,0:T(8,128)S(1)} fusion(f32[16,1024]{0,1:T(8,128)S(1)} %bitcast.219, s32[1024]{0:T(1024)S(1)} %broadcast_clamp_fusion.4), kind=kCustom, calls=%fused_computation.5 | custom fusion | bytes 135168 | tf_op jit(solution)/shard_map/gather | solution.py:101
  130.3 8.4 %fusion.66 = f32[16,4,1,128]{3,2,1,0:T(1,128)S(1)} fusion(f32[16,4,128,1]{2,3,1,0:T(1,128)S(1)} %copy.145, f32[16,4,128,128]{3,2,1,0:T(8,128)} %param.16), kind=kOutput, calls=%fused_computation.148 | convolution fusion | flops 12582912 | bytes 4259840 | tf_op jit(solution)/shard_map/mnij,mnj->mni/dot_general | solution.py:108
  140.8 3.4 %fusion.67 = f32[16,2,1,128]{3,2,1,0:T(1,128)S(1)} fusion(f32[16,2,128,1]{2,3,1,0:T(1,128)S(1)} %bitcast.248, f32[16,2,128,128]{3,2,1,0:T(8,128)S(1)} %copy-done), kind=kOutput, calls=%fused_computation.149 | convolution fusion | flops 6291456 | bytes 2129920 | tf_op jit(solution)/shard_map/mnij,mnj->mni/dot_general | solution.py:108
  152.8 3.7 %fusion.69 = f32[16,4,1,128]{3,2,1,0:T(1,128)S(1)} fusion(f32[16,4,128,1]{2,3,1,0:T(1,128)S(1)} %bitcast.243, f32[16,4,128,128]{3,2,1,0:T(8,128)S(1)} %copy-done.1), kind=kOutput, calls=%fused_computation.151 | convolution fusion | flops 12582912 | bytes 4259840 | tf_op jit(solution)/shard_map/mnji,mnj->mni/dot_general | solution.py:117
  158.3 3.6 %scatter_custom_fusion.1 = f32[16,1024]{0,1:T(8,128)S(1)} fusion(s32[1024]{0:T(1024)} %bitcast.263, f32[16,1024]{0,1:T(8,128)S(1)} %fusion.9, f32[]{:T(128)} %constant.79.clone.1), kind=kCustom, calls=%fused_computation.22 | custom fusion | bytes 131584 | tf_op jit(solution)/shard_map/scatter | solution.py:122
  162.1 9.3 %all_to_all.66 = f32[16,8,128]{2,0,1:T(8,128)S(1)} all-to-all(f32[16,8,128]{2,0,1:T(8,128)S(1)} %copy.133), channel_id=1, replica_groups=mesh['case'=2,'span'=8,'dom'=2] {'span'}, dimensions={1} | all-to-all | bytes 131072 | tf_op jit(solution)/shard_map/all_to_all | solution.py:124
  173.6 10.9 %all_to_all.67 = f32[8,16,512]{2,1,0:T(8,128)S(1)} all-to-all(f32[8,16,512]{2,1,0:T(8,128)S(1)} %bitcast.224), channel_id=1, replica_groups=mesh['case'=2,'span'=8,'dom'=2] {'span'}, dimensions={0} | all-to-all | bytes 524288 | tf_op jit(solution)/shard_map/all_to_all | solution.py:127
  186.5 3.4 %collective-permute-start.5 = (f32[1,4096]{1,0:T(1,128)}, f32[1,4096]{1,0:T(1,128)}, u32[]{:S(2)}, u32[]{:S(2)}) collective-permute-start(f32[1,4096]{1,0:T(1,128)} %bitcast.76), channel_id=1, source_target_pairs={{2,0},{4,2},{6,4},{8,6},{10,8},{12,10},{14,12},{0,14},{3,1},{5,3},... | collective-permute-start | bytes 49160 | tf_op jit(solution)/shard_map/ppermute | solution.py:21
  191.3 3.0 %collective-permute-start.7 = (f32[16,64]{1,0:T(8,128)S(1)}, f32[16,64]{1,0:T(8,128)S(1)}, u32[]{:S(2)}, u32[]{:S(2)}) collective-permute-start(f32[16,64]{1,0:T(8,128)S(1)} %get-tuple-element.15), channel_id=1, source_target_pairs={{0,1},{2,3},{4,5},{6,7},{8,9},{10,11},{12,13},{14,15},{16,17},{18,... | collective-permute-start | bytes 12296 | tf_op jit(solution)/shard_map/ppermute | solution.py:20
  197.3 15.7 %gather_fusion.9 = f32[4096,16]{1,0:T(8,128)} fusion(f32[16,4224]{0,1:T(8,128)} %copy.137, s32[4096]{0:T(1024)S(1)} %broadcast_clamp_fusion), kind=kCustom, calls=%fused_computation.9 | custom fusion | bytes 540672 | tf_op jit(solution)/shard_map/gather | solution.py:50
  213.0 15.7 %gather_fusion.8 = f32[4096,16]{1,0:T(8,128)} fusion(f32[16,4224]{0,1:T(8,128)} %copy.137, s32[4096]{0:T(1024)S(1)} %broadcast_clamp_fusion.1), kind=kCustom, calls=%fused_computation.8 | custom fusion | bytes 540672 | tf_op jit(solution)/shard_map/gather | solution.py:50
  228.7 15.7 %gather_fusion.7 = f32[4096,16]{1,0:T(8,128)} fusion(f32[16,4224]{0,1:T(8,128)} %copy.137, s32[4096]{0:T(1024)S(1)} %broadcast_clamp_fusion.2), kind=kCustom, calls=%fused_computation.7 | custom fusion | bytes 540672 | tf_op jit(solution)/shard_map/gather | solution.py:50
  244.4 15.7 %gather_fusion.6 = f32[4096,16]{1,0:T(8,128)} fusion(f32[16,4224]{0,1:T(8,128)} %copy.137, s32[4096]{0:T(1024)S(1)} %broadcast_clamp_fusion.3), kind=kCustom, calls=%fused_computation.6 | custom fusion | bytes 540672 | tf_op jit(solution)/shard_map/gather | solution.py:50
  262.2 2.2 copy.142
  264.4 2.2 copy.140
  266.6 2.9 %copy.138 = f32[4096,16]{0,1:T(8,128)} copy(f32[4096,16]{1,0:T(8,128)} %gather_fusion.6) | data formatting | bytes 524288 | tf_op jit(solution)/shard_map/gather | solution.py:50
  (117 shorter events, 45.0 us)
Async XLA Ops:
  0.6 140.2 %copy-start = (f32[16,2,128,128]{3,2,1,0:T(8,128)S(1)}, f32[16,2,128,128]{3,2,1,0:T(8,128)}, u32[]{:S(2)}) copy-start(f32[16,2,128,128]{3,2,1,0:T(8,128)} %param.17) | copy-start | bytes 6291460
  1.6 20.0 %collective-permute-start.3 = (f32[16,64]{1,0:T(8,128)S(1)}, f32[16,64]{1,0:T(8,128)S(1)}, u32[]{:S(2)}, u32[]{:S(2)}) collective-permute-start(f32[16,64]{1,0:T(8,128)S(1)} %get-tuple-element.18), channel_id=1, source_target_pairs={{1,0},{3,2},{5,4},{7,6},{9,8},{11,10},{13,12},{15,14},{17,16},{19,... | collective-permute-start | bytes 12296 | tf_op jit(solution)/shard_map/ppermute | solution.py:21
  2.9 18.7 %collective-permute-start.2 = (f32[16,64]{1,0:T(8,128)S(1)}, f32[16,64]{1,0:T(8,128)S(1)}, u32[]{:S(2)}, u32[]{:S(2)}) collective-permute-start(f32[16,64]{1,0:T(8,128)S(1)} %get-tuple-element.19), channel_id=1, source_target_pairs={{0,1},{2,3},{4,5},{6,7},{8,9},{10,11},{12,13},{14,15},{16,17},{18,... | collective-permute-start | bytes 12296 | tf_op jit(solution)/shard_map/ppermute | solution.py:20
  7.5 89.5 %collective-permute-start = (f32[1,4096]{1,0:T(1,128)}, f32[1,4096]{1,0:T(1,128)S(1)}, u32[]{:S(2)}, u32[]{:S(2)}) collective-permute-start(f32[1,4096]{1,0:T(1,128)} %get-tuple-element.20), channel_id=1, source_target_pairs={{2,0},{4,2},{6,4},{8,6},{10,8},{12,10},{14,12},{0,14},{3,1},{5,3},... | collective-permute-start | bytes 49160 | tf_op jit(solution)/shard_map/ppermute | solution.py:21
  13.5 83.5 %collective-permute-start.1 = (f32[1,4096]{1,0:T(1,128)}, f32[1,4096]{1,0:T(1,128)}, u32[]{:S(2)}, u32[]{:S(2)}) collective-permute-start(f32[1,4096]{1,0:T(1,128)} %get-tuple-element.21), channel_id=1, source_target_pairs={{0,2},{2,4},{4,6},{6,8},{8,10},{10,12},{12,14},{14,0},{1,3},{3,5},... | collective-permute-start | bytes 49160 | tf_op jit(solution)/shard_map/ppermute | solution.py:20
  21.0 76.0 %copy-start.10 = (f32[1,4096]{1,0:T(1,128)}, f32[1,4096]{1,0:T(1,128)S(1)}, u32[]{:S(2)}) copy-start(f32[1,4096]{1,0:T(1,128)S(1)} %get-tuple-element.25) | copy-start | bytes 49156
  78.3 18.7 %copy-start.4 = (f32[16,4096]{1,0:T(8,128)S(1)}, f32[16,4096]{1,0:T(8,128)}, u32[]{:S(2)}) copy-start(f32[16,4096]{1,0:T(8,128)} %param.10) | copy-start | bytes 786436
  78.3 18.7 %copy-start.9 = (f32[16,4096]{1,0:T(8,128)S(1)}, f32[16,4096]{1,0:T(8,128)}, u32[]{:S(2)}) copy-start(f32[16,4096]{1,0:T(8,128)} %param.11) | copy-start | bytes 786436
  98.2 21.4 %copy-start.12 = (s32[1024,1]{0,1:T(1,128)S(1)}, s32[1024,1]{0,1:T(1,128)}, u32[]{:S(2)}) copy-start(s32[1024,1]{0,1:T(1,128)} %get-tuple-element.10) | copy-start | bytes 12292
  98.9 14.2 %all-to-all-start = ((f32[16,8,512]{2,0,1:T(8,128)}), f32[16,8,512]{2,0,1:T(8,128)S(1)}, u32[]{:S(2)}, u32[]{:S(2)}) async-start(f32[16,8,512]{2,0,1:T(8,128)} %bitcast.210), calls=%async_computation | async-start | bytes 524288 | tf_op jit(solution)/shard_map/all_to_all | solution.py:84
  104.9 24.6 %copy-start.14 = (s32[128]{0:T(128)}, s32[128]{0:T(128)S(1)}, u32[]{:S(2)}) copy-start(s32[128]{0:T(128)S(1)} %add_select_fusion.3) | copy-start | bytes 1540
  110.2 19.3 %copy-start.16 = (f32[128]{0:T(128)}, f32[128]{0:T(128)S(1)}, u32[]{:S(2)}) copy-start(f32[128]{0:T(128)S(1)} %get-tuple-element.32) | copy-start | bytes 1540
  116.0 10.5 %all-to-all-start.1 = ((f32[8,16,128]{2,1,0:T(8,128)}), f32[8,16,128]{2,1,0:T(8,128)S(1)}, u32[]{:S(2)}, u32[]{:S(2)}) async-start(f32[8,16,128]{2,1,0:T(8,128)} %bitcast.26), calls=%async_computation.1 | async-start | bytes 131072 | tf_op jit(solution)/shard_map/all_to_all | solution.py:100
  129.5 0.8 copy-start.7
  138.7 8.4 %copy-start.2 = (f32[16,1,128,128]{3,2,1,0:T(8,128)S(1)}, f32[16,1,128,128]{3,2,1,0:T(8,128)}, u32[]{:S(2)}) copy-start(f32[16,1,128,128]{3,2,1,0:T(8,128)} %param.19) | copy-start | bytes 3145732
  140.0 4.2 %copy-start.3 = (f32[16,1,128,128]{3,2,1,0:T(8,128)S(1)}, f32[16,1,128,128]{3,2,1,0:T(8,128)}, u32[]{:S(2)}) copy-start(f32[16,1,128,128]{3,2,1,0:T(8,128)} %param.18) | copy-start | bytes 3145732
  145.9 1.2 collective-permute-start.4
  148.9 3.9 %copy-start.1 = (f32[16,4,128,128]{3,2,1,0:T(8,128)S(1)}, f32[16,4,128,128]{3,2,1,0:T(8,128)}, u32[]{:S(2)}) copy-start(f32[16,4,128,128]{3,2,1,0:T(8,128)} %param.16) | copy-start | bytes 12582916
  152.8 4.5 %copy-start.8 = (f32[1024,16]{1,0:T(8,128)S(1)}, f32[1024,16]{1,0:T(8,128)}, u32[]{:S(2)}) copy-start(f32[1024,16]{1,0:T(8,128)} %copy-done.7) | copy-start | bytes 196612
  156.4 15.0 %copy-start.18 = (s32[128]{0:T(128)S(1)}, s32[128]{0:T(128)}, u32[]{:S(2)}) copy-start(s32[128]{0:T(128)} %get-tuple-element.31) | copy-start | bytes 1540
  157.3 15.6 %copy-start.13 = (pred[128]{0:T(512)(128)(4,1)S(1)}, pred[128]{0:T(512)(128)(4,1)}, u32[]{:S(2)}) copy-start(pred[128]{0:T(512)(128)(4,1)} %iota_compare_fusion.2) | copy-start | bytes 388
  157.3 15.6 %copy-start.15 = (s32[128]{0:T(128)S(1)}, s32[128]{0:T(128)}, u32[]{:S(2)}) copy-start(s32[128]{0:T(128)} %copy-done.14) | copy-start | bytes 1540
  157.3 15.6 %copy-start.17 = (f32[128]{0:T(128)S(1)}, f32[128]{0:T(128)}, u32[]{:S(2)}) copy-start(f32[128]{0:T(128)} %copy-done.16) | copy-start | bytes 1540
  185.2 84.3 %collective-permute-start.6 = (f32[1,4096]{1,0:T(1,128)}, f32[1,4096]{1,0:T(1,128)S(1)}, u32[]{:S(2)}, u32[]{:S(2)}) collective-permute-start(f32[1,4096]{1,0:T(1,128)} %bitcast.77), channel_id=1, source_target_pairs={{0,2},{2,4},{4,6},{6,8},{8,10},{10,12},{12,14},{14,0},{1,3},{3,5},... | collective-permute-start | bytes 49160 | tf_op jit(solution)/shard_map/ppermute | solution.py:20
  186.5 83.0 %collective-permute-start.5 = (f32[1,4096]{1,0:T(1,128)}, f32[1,4096]{1,0:T(1,128)}, u32[]{:S(2)}, u32[]{:S(2)}) collective-permute-start(f32[1,4096]{1,0:T(1,128)} %bitcast.76), channel_id=1, source_target_pairs={{2,0},{4,2},{6,4},{8,6},{10,8},{12,10},{14,12},{0,14},{3,1},{5,3},... | collective-permute-start | bytes 49160 | tf_op jit(solution)/shard_map/ppermute | solution.py:21
  189.9 79.6 %copy-start.6 = (f32[8,2,8,512]{3,2,0,1:T(8,128)}, f32[8,2,8,512]{3,2,0,1:T(8,128)S(1)}, u32[]{:S(2)}) copy-start(f32[8,2,8,512]{3,2,0,1:T(8,128)S(1)} %copy.162) | copy-start | bytes 786436
  190.0 4.3 %collective-permute-start.8 = (f32[16,64]{1,0:T(8,128)S(1)}, f32[16,64]{1,0:T(8,128)S(1)}, u32[]{:S(2)}, u32[]{:S(2)}) collective-permute-start(f32[16,64]{1,0:T(8,128)S(1)} %get-tuple-element.14), channel_id=1, source_target_pairs={{1,0},{3,2},{5,4},{7,6},{9,8},{11,10},{13,12},{15,14},{17,16},{19,... | collective-permute-start | bytes 12296 | tf_op jit(solution)/shard_map/ppermute | solution.py:21
  191.3 3.8 %collective-permute-start.7 = (f32[16,64]{1,0:T(8,128)S(1)}, f32[16,64]{1,0:T(8,128)S(1)}, u32[]{:S(2)}, u32[]{:S(2)}) collective-permute-start(f32[16,64]{1,0:T(8,128)S(1)} %get-tuple-element.15), channel_id=1, source_target_pairs={{0,1},{2,3},{4,5},{6,7},{8,9},{10,11},{12,13},{14,15},{16,17},{18,... | collective-permute-start | bytes 12296 | tf_op jit(solution)/shard_map/ppermute | solution.py:20
  264.4 5.1 %copy-start.5 = (f32[16,4096]{1,0:T(8,128)S(1)}, f32[16,4096]{1,0:T(8,128)}, u32[]{:S(2)}) copy-start(f32[16,4096]{1,0:T(8,128)} %param.10) | copy-start | bytes 786436
  264.4 5.1 %copy-start.11 = (f32[1,4096]{1,0:T(1,128)S(1)}, f32[1,4096]{1,0:T(1,128)}, u32[]{:S(2)}) copy-start(f32[1,4096]{1,0:T(1,128)} %copy-done.10) | copy-start | bytes 49156
where the time goes:
time: 273 us; the launch traced here: 271 us
  local copies, waits for them, and re-layouts  172 us (63%)
  starting transfers between devices  28.9 us (11%)
  matrix products  24.8 us (9%)
  blocking collectives  20.2 us (7%)
  other arithmetic  13.5 us (5%)
  waiting for transfers between devices  11.3 us (4%)
    gather x16, local copies, waits for them, and re-layouts, stencil(): widened[:, near_local[slot]] - field  144 us
    dot_general x3, matrix products, on_device(): jnp.einsum('mnij,mnj->mni', blocks, paired, precision=lax.Precision.HIGHEST)  13.5 us
    ppermute x4, starting transfers between devices, extended(): after = lax.ppermute(initial, axis, down)  12 us
    all_to_all x1, blocking collectives, on_device(): lax.all_to_all(pressure_cols, 'span', split_axis=0, concat_axis=1, tiled=...  10.9 us
    all_to_all x1, blocking collectives, on_device(): lax.all_to_all(outgoing, 'span', split_axis=1, concat_axis=0, tiled=True)  9.29 us
    ppermute x4, starting transfers between devices, extended(): before = lax.ppermute(last, axis, up)  7.37 us
    all_to_all x1, waiting for transfers between devices, on_device(): lax.all_to_all(payload, 'span', split_axis=0, concat_axis=1, tiled=True)  6.89 us
    dot_general x3, matrix products, on_device(): jnp.einsum('mnji,mnj->mni', blocks, lowered, precision=lax.Precision.HIGH...  6.5 us
  transfers between devices with their start and end apart: 11, of which 4 were waited for; matrix products, arithmetic and copies ran while one was open for 61% of the time, Pallas kernels for 0%

commit v1 on v0

--- a/solution.py
+++ b/solution.py
@@ -87,8 +87,9 @@
     interior_cols = spectrum_cols / (diag_cols[None, :] + wave_shift(all_waves)[:, None])
     flat_iface = local_iface.reshape(-1)
     owner = flat_iface // cols_count
-    onehot = (owner[:, None] == jnp.arange(span_count, dtype=jnp.int32)[None, :]).astype(jnp.int32)
-    ranks = jnp.sum(jnp.cumsum(onehot, 0) * onehot, 1) - 1
+    order = jnp.arange(flat_iface.shape[0], dtype=jnp.int32)
+    earlier = (owner[:, None] == owner[None, :]) & (order[None, :] < order[:, None])
+    ranks = jnp.sum(earlier.astype(jnp.int32), 1)
     slot_index = owner * slot_count + ranks
     owned = owner == span_pos
     slot_cell = (

time: 273 us -> 271 us (level)
  no operation moved by 1% of the time
where the time goes in v1:
time: 271 us; the launch traced here: 270 us
  local copies, waits for them, and re-layouts  172 us (63%)
  starting transfers between devices  29 us (11%)
  matrix products  24.7 us (9%)
  blocking collectives  20.2 us (7%)
  other arithmetic  11.5 us (4%)
  waiting for transfers between devices  11.2 us (4%)
    gather x16, local copies, waits for them, and re-layouts, stencil(): widened[:, near_local[slot]] - field  145 us
    dot_general x3, matrix products, on_device(): jnp.einsum('mnij,mnj->mni', blocks, paired, precision=lax.Precision.HIGHEST)  13.5 us
    ppermute x4, starting transfers between devices, extended(): after = lax.ppermute(initial, axis, down)  12 us
    all_to_all x1, blocking collectives, on_device(): lax.all_to_all(pressure_cols, 'span', split_axis=0, concat_axis=1, tiled=...  10.9 us
    all_to_all x1, blocking collectives, on_device(): lax.all_to_all(outgoing, 'span', split_axis=1, concat_axis=0, tiled=True)  9.29 us
    ppermute x4, starting transfers between devices, extended(): before = lax.ppermute(last, axis, up)  7.37 us
    all_to_all x1, waiting for transfers between devices, on_device(): lax.all_to_all(payload, 'span', split_axis=0, concat_axis=1, tiled=True)  6.89 us
    dot_general x3, matrix products, on_device(): jnp.einsum('mnji,mnj->mni', blocks, lowered, precision=lax.Precision.HIGH...  6.5 us
  transfers between devices with their start and end apart: 11, of which 4 were waited for; matrix products, arithmetic and copies ran while one was open for 61% of the time, Pallas kernels for 0%

profile of v1, /device:TPU:0, one launch (start us, length us, event | category | flops | bytes accessed | tf_op | source)
XLA Modules:
  0.0 269.8 jit_solution(4078936180641892087)
XLA Ops:
  2.9 3.0 %collective-permute-start.2 = (f32[16,64]{1,0:T(8,128)S(1)}, f32[16,64]{1,0:T(8,128)S(1)}, u32[]{:S(2)}, u32[]{:S(2)}) collective-permute-start(f32[16,64]{1,0:T(8,128)S(1)} %get-tuple-element.19), channel_id=1, source_target_pairs={{0,1},{2,3},{4,5},{6,7},{8,9},{10,11},{12,13},{14,15},{16,17},{18,... | collective-permute-start | bytes 12296 | tf_op jit(solution)/shard_map/ppermute | solution.py:20
  7.5 6.0 %collective-permute-start = (f32[1,4096]{1,0:T(1,128)}, f32[1,4096]{1,0:T(1,128)S(1)}, u32[]{:S(2)}, u32[]{:S(2)}) collective-permute-start(f32[1,4096]{1,0:T(1,128)} %get-tuple-element.20), channel_id=1, source_target_pairs={{2,0},{4,2},{6,4},{8,6},{10,8},{12,10},{14,12},{0,14},{3,1},{5,3},... | collective-permute-start | bytes 49160 | tf_op jit(solution)/shard_map/ppermute | solution.py:21
  22.3 15.8 %gather_fusion.3 = f32[4096,16]{1,0:T(8,128)} fusion(f32[16,4224]{0,1:T(8,128)} %copy.121, s32[4096]{0:T(1024)S(1)} %broadcast_clamp_fusion), kind=kCustom, calls=%fused_computation.3 | custom fusion | bytes 540672 | tf_op jit(solution)/shard_map/gather | solution.py:50
  38.0 2.2 copy.128
  40.2 15.8 %gather_fusion.2 = f32[4096,16]{1,0:T(8,128)} fusion(f32[16,4224]{0,1:T(8,128)} %copy.121, s32[4096]{0:T(1024)S(1)} %broadcast_clamp_fusion.1), kind=kCustom, calls=%fused_computation.2 | custom fusion | bytes 540672 | tf_op jit(solution)/shard_map/gather | solution.py:50
  56.0 2.2 copy.126
  58.1 15.8 %gather_fusion.1 = f32[4096,16]{1,0:T(8,128)} fusion(f32[16,4224]{0,1:T(8,128)} %copy.121, s32[4096]{0:T(1024)S(1)} %broadcast_clamp_fusion.2), kind=kCustom, calls=%fused_computation.1 | custom fusion | bytes 540672 | tf_op jit(solution)/shard_map/gather | solution.py:50
  73.9 2.2 copy.124
  76.1 15.8 %gather_fusion = f32[4096,16]{1,0:T(8,128)} fusion(f32[16,4224]{0,1:T(8,128)} %copy.121, s32[4096]{0:T(1024)S(1)} %broadcast_clamp_fusion.3), kind=kCustom, calls=%fused_computation | custom fusion | bytes 540672 | tf_op jit(solution)/shard_map/gather | solution.py:50
  91.9 2.9 %copy.122 = f32[4096,16]{0,1:T(8,128)} copy(f32[4096,16]{1,0:T(8,128)} %gather_fusion) | data formatting | bytes 524288 | tf_op jit(solution)/shard_map/gather | solution.py:50
  96.7 6.0 %all-to-all-start = ((f32[16,8,512]{2,0,1:T(8,128)}), f32[16,8,512]{2,0,1:T(8,128)S(1)}, u32[]{:S(2)}, u32[]{:S(2)}) async-start(f32[16,8,512]{2,0,1:T(8,128)} %bitcast.196), calls=%async_computation | async-start | bytes 524288 | tf_op jit(solution)/shard_map/all_to_all | solution.py:84
  103.5 4.4 %scatter_custom_fusion = s32[128]{0:T(128)S(1)} fusion(s32[1024]{0:T(1024)} %bitcast.249, s32[1024]{0:T(1024)} %get-tuple-element.12, s32[]{:T(128)} %constant.66.clone.1), kind=kCustom, calls=%fused_computation.120 | custom fusion | bytes 1024 | tf_op jit(solution)/shard_map/scatter | solution.py:98
  108.6 2.3 all-to-all-done
  113.7 3.7 %all-to-all-start.1 = ((f32[8,16,128]{2,1,0:T(8,128)}), f32[8,16,128]{2,1,0:T(8,128)S(1)}, u32[]{:S(2)}, u32[]{:S(2)}) async-start(f32[8,16,128]{2,1,0:T(8,128)} %bitcast.25), calls=%async_computation.1 | async-start | bytes 131072 | tf_op jit(solution)/shard_map/all_to_all | solution.py:101
  117.4 6.9 %all-to-all-done.1 = f32[8,16,128]{2,1,0:T(8,128)S(1)} async-done(((f32[8,16,128]{2,1,0:T(8,128)}), f32[8,16,128]{2,1,0:T(8,128)S(1)}, u32[]{:S(2)}, u32[]{:S(2)}) %all-to-all-start.1) | async-done | bytes 65568 | tf_op jit(solution)/shard_map/all_to_all | solution.py:101
  124.5 2.8 %gather_fusion.5 = f32[1024,16]{1,0:T(8,128)S(1)} fusion(f32[16,1024]{0,1:T(8,128)S(1)} %bitcast.204, s32[1024]{0:T(1024)S(1)} %broadcast_clamp_fusion.4), kind=kCustom, calls=%fused_computation.5 | custom fusion | bytes 135168 | tf_op jit(solution)/shard_map/gather | solution.py:102
  128.1 8.4 %fusion.62 = f32[16,4,1,128]{3,2,1,0:T(1,128)S(1)} fusion(f32[16,4,128,1]{2,3,1,0:T(1,128)S(1)} %copy.145, f32[16,4,128,128]{3,2,1,0:T(8,128)} %param.16), kind=kOutput, calls=%fused_computation.135 | convolution fusion | flops 12582912 | bytes 4259840 | tf_op jit(solution)/shard_map/mnij,mnj->mni/dot_general | solution.py:109
  138.7 3.4 %fusion.63 = f32[16,2,1,128]{3,2,1,0:T(1,128)S(1)} fusion(f32[16,2,128,1]{2,3,1,0:T(1,128)S(1)} %bitcast.233, f32[16,2,128,128]{3,2,1,0:T(8,128)S(1)} %copy-done), kind=kOutput, calls=%fused_computation.136 | convolution fusion | flops 6291456 | bytes 2129920 | tf_op jit(solution)/shard_map/mnij,mnj->mni/dot_general | solution.py:109
  150.6 3.7 %fusion.65 = f32[16,4,1,128]{3,2,1,0:T(1,128)S(1)} fusion(f32[16,4,128,1]{2,3,1,0:T(1,128)S(1)} %bitcast.228, f32[16,4,128,128]{3,2,1,0:T(8,128)S(1)} %copy-done.1), kind=kOutput, calls=%fused_computation.138 | convolution fusion | flops 12582912 | bytes 4259840 | tf_op jit(solution)/shard_map/mnji,mnj->mni/dot_general | solution.py:118
  156.2 3.6 %scatter_custom_fusion.1 = f32[16,1024]{0,1:T(8,128)S(1)} fusion(s32[1024]{0:T(1024)} %bitcast.247, f32[16,1024]{0,1:T(8,128)S(1)} %fusion.10, f32[]{:T(128)} %constant.73.clone.1), kind=kCustom, calls=%fused_computation.25 | custom fusion | bytes 131584 | tf_op jit(solution)/shard_map/scatter | solution.py:123
  159.9 9.3 %all_to_all.66 = f32[16,8,128]{2,0,1:T(8,128)S(1)} all-to-all(f32[16,8,128]{2,0,1:T(8,128)S(1)} %copy.133), channel_id=1, replica_groups=mesh['case'=2,'span'=8,'dom'=2] {'span'}, dimensions={1} | all-to-all | bytes 131072 | tf_op jit(solution)/shard_map/all_to_all | solution.py:125
  171.5 10.9 %all_to_all.67 = f32[8,16,512]{2,1,0:T(8,128)S(1)} all-to-all(f32[8,16,512]{2,1,0:T(8,128)S(1)} %bitcast.209), channel_id=1, replica_groups=mesh['case'=2,'span'=8,'dom'=2] {'span'}, dimensions={0} | all-to-all | bytes 524288 | tf_op jit(solution)/shard_map/all_to_all | solution.py:128
  184.4 3.4 %collective-permute-start.5 = (f32[1,4096]{1,0:T(1,128)}, f32[1,4096]{1,0:T(1,128)}, u32[]{:S(2)}, u32[]{:S(2)}) collective-permute-start(f32[1,4096]{1,0:T(1,128)} %bitcast.75), channel_id=1, source_target_pairs={{2,0},{4,2},{6,4},{8,6},{10,8},{12,10},{14,12},{0,14},{3,1},{5,3},... | collective-permute-start | bytes 49160 | tf_op jit(solution)/shard_map/ppermute | solution.py:21
  189.2 3.0 %collective-permute-start.7 = (f32[16,64]{1,0:T(8,128)S(1)}, f32[16,64]{1,0:T(8,128)S(1)}, u32[]{:S(2)}, u32[]{:S(2)}) collective-permute-start(f32[16,64]{1,0:T(8,128)S(1)} %get-tuple-element.15), channel_id=1, source_target_pairs={{0,1},{2,3},{4,5},{6,7},{8,9},{10,11},{12,13},{14,15},{16,17},{18,... | collective-permute-start | bytes 12296 | tf_op jit(solution)/shard_map/ppermute | solution.py:20
  195.2 15.8 %gather_fusion.9 = f32[4096,16]{1,0:T(8,128)} fusion(f32[16,4224]{0,1:T(8,128)} %copy.137, s32[4096]{0:T(1024)S(1)} %broadcast_clamp_fusion), kind=kCustom, calls=%fused_computation.9 | custom fusion | bytes 540672 | tf_op jit(solution)/shard_map/gather | solution.py:50
  211.0 15.8 %gather_fusion.8 = f32[4096,16]{1,0:T(8,128)} fusion(f32[16,4224]{0,1:T(8,128)} %copy.137, s32[4096]{0:T(1024)S(1)} %broadcast_clamp_fusion.1), kind=kCustom, calls=%fused_computation.8 | custom fusion | bytes 540672 | tf_op jit(solution)/shard_map/gather | solution.py:50
  226.8 15.8 %gather_fusion.7 = f32[4096,16]{1,0:T(8,128)} fusion(f32[16,4224]{0,1:T(8,128)} %copy.137, s32[4096]{0:T(1024)S(1)} %broadcast_clamp_fusion.2), kind=kCustom, calls=%fused_computation.7 | custom fusion | bytes 540672 | tf_op jit(solution)/shard_map/gather | solution.py:50
  242.6 15.8 %gather_fusion.6 = f32[4096,16]{1,0:T(8,128)} fusion(f32[16,4224]{0,1:T(8,128)} %copy.137, s32[4096]{0:T(1024)S(1)} %broadcast_clamp_fusion.3), kind=kCustom, calls=%fused_computation.6 | custom fusion | bytes 540672 | tf_op jit(solution)/shard_map/gather | solution.py:50
  258.4 2.2 copy.144
  260.6 2.2 copy.142
  262.8 2.2 copy.140
  265.0 2.9 %copy.138 = f32[4096,16]{0,1:T(8,128)} copy(f32[4096,16]{1,0:T(8,128)} %gather_fusion.6) | data formatting | bytes 524288 | tf_op jit(solution)/shard_map/gather | solution.py:50
  (110 shorter events, 42.8 us)
Async XLA Ops:
  0.6 138.0 %copy-start = (f32[16,2,128,128]{3,2,1,0:T(8,128)S(1)}, f32[16,2,128,128]{3,2,1,0:T(8,128)}, u32[]{:S(2)}) copy-start(f32[16,2,128,128]{3,2,1,0:T(8,128)} %param.17) | copy-start | bytes 6291460
  1.6 17.5 %collective-permute-start.3 = (f32[16,64]{1,0:T(8,128)S(1)}, f32[16,64]{1,0:T(8,128)S(1)}, u32[]{:S(2)}, u32[]{:S(2)}) collective-permute-start(f32[16,64]{1,0:T(8,128)S(1)} %get-tuple-element.18), channel_id=1, source_target_pairs={{1,0},{3,2},{5,4},{7,6},{9,8},{11,10},{13,12},{15,14},{17,16},{19,... | collective-permute-start | bytes 12296 | tf_op jit(solution)/shard_map/ppermute | solution.py:21
  2.9 16.3 %collective-permute-start.2 = (f32[16,64]{1,0:T(8,128)S(1)}, f32[16,64]{1,0:T(8,128)S(1)}, u32[]{:S(2)}, u32[]{:S(2)}) collective-permute-start(f32[16,64]{1,0:T(8,128)S(1)} %get-tuple-element.19), channel_id=1, source_target_pairs={{0,1},{2,3},{4,5},{6,7},{8,9},{10,11},{12,13},{14,15},{16,17},{18,... | collective-permute-start | bytes 12296 | tf_op jit(solution)/shard_map/ppermute | solution.py:20
  7.5 87.3 %collective-permute-start = (f32[1,4096]{1,0:T(1,128)}, f32[1,4096]{1,0:T(1,128)S(1)}, u32[]{:S(2)}, u32[]{:S(2)}) collective-permute-start(f32[1,4096]{1,0:T(1,128)} %get-tuple-element.20), channel_id=1, source_target_pairs={{2,0},{4,2},{6,4},{8,6},{10,8},{12,10},{14,12},{0,14},{3,1},{5,3},... | collective-permute-start | bytes 49160 | tf_op jit(solution)/shard_map/ppermute | solution.py:21
  13.5 81.3 %collective-permute-start.1 = (f32[1,4096]{1,0:T(1,128)}, f32[1,4096]{1,0:T(1,128)}, u32[]{:S(2)}, u32[]{:S(2)}) collective-permute-start(f32[1,4096]{1,0:T(1,128)} %get-tuple-element.21), channel_id=1, source_target_pairs={{0,2},{2,4},{4,6},{6,8},{8,10},{10,12},{12,14},{14,0},{1,3},{3,5},... | collective-permute-start | bytes 49160 | tf_op jit(solution)/shard_map/ppermute | solution.py:20
  18.6 76.2 %copy-start.10 = (f32[1,4096]{1,0:T(1,128)}, f32[1,4096]{1,0:T(1,128)S(1)}, u32[]{:S(2)}) copy-start(f32[1,4096]{1,0:T(1,128)S(1)} %get-tuple-element.25) | copy-start | bytes 49156
  76.1 18.7 %copy-start.4 = (f32[16,4096]{1,0:T(8,128)S(1)}, f32[16,4096]{1,0:T(8,128)}, u32[]{:S(2)}) copy-start(f32[16,4096]{1,0:T(8,128)} %param.10) | copy-start | bytes 786436
  76.1 18.7 %copy-start.9 = (f32[16,4096]{1,0:T(8,128)S(1)}, f32[16,4096]{1,0:T(8,128)}, u32[]{:S(2)}) copy-start(f32[16,4096]{1,0:T(8,128)} %param.11) | copy-start | bytes 786436
  96.0 21.4 %copy-start.12 = (s32[1024,1]{0,1:T(1,128)S(1)}, s32[1024,1]{0,1:T(1,128)}, u32[]{:S(2)}) copy-start(s32[1024,1]{0,1:T(1,128)} %get-tuple-element.10) | copy-start | bytes 12292
  96.7 14.2 %all-to-all-start = ((f32[16,8,512]{2,0,1:T(8,128)}), f32[16,8,512]{2,0,1:T(8,128)S(1)}, u32[]{:S(2)}, u32[]{:S(2)}) async-start(f32[16,8,512]{2,0,1:T(8,128)} %bitcast.196), calls=%async_computation | async-start | bytes 524288 | tf_op jit(solution)/shard_map/all_to_all | solution.py:84
  102.7 24.6 %copy-start.14 = (s32[128]{0:T(128)}, s32[128]{0:T(128)S(1)}, u32[]{:S(2)}) copy-start(s32[128]{0:T(128)S(1)} %add_select_fusion.2) | copy-start | bytes 1540
  108.0 19.4 %copy-start.16 = (f32[128]{0:T(128)}, f32[128]{0:T(128)S(1)}, u32[]{:S(2)}) copy-start(f32[128]{0:T(128)S(1)} %get-tuple-element.32) | copy-start | bytes 1540
  113.7 10.6 %all-to-all-start.1 = ((f32[8,16,128]{2,1,0:T(8,128)}), f32[8,16,128]{2,1,0:T(8,128)S(1)}, u32[]{:S(2)}, u32[]{:S(2)}) async-start(f32[8,16,128]{2,1,0:T(8,128)} %bitcast.25), calls=%async_computation.1 | async-start | bytes 131072 | tf_op jit(solution)/shard_map/all_to_all | solution.py:101
  127.3 0.8 copy-start.7
  136.6 8.4 %copy-start.2 = (f32[16,1,128,128]{3,2,1,0:T(8,128)S(1)}, f32[16,1,128,128]{3,2,1,0:T(8,128)}, u32[]{:S(2)}) copy-start(f32[16,1,128,128]{3,2,1,0:T(8,128)} %param.19) | copy-start | bytes 3145732
  137.8 4.2 %copy-start.3 = (f32[16,1,128,128]{3,2,1,0:T(8,128)S(1)}, f32[16,1,128,128]{3,2,1,0:T(8,128)}, u32[]{:S(2)}) copy-start(f32[16,1,128,128]{3,2,1,0:T(8,128)} %param.18) | copy-start | bytes 3145732
  143.8 1.2 collective-permute-start.4
  146.7 3.9 %copy-start.1 = (f32[16,4,128,128]{3,2,1,0:T(8,128)S(1)}, f32[16,4,128,128]{3,2,1,0:T(8,128)}, u32[]{:S(2)}) copy-start(f32[16,4,128,128]{3,2,1,0:T(8,128)} %param.16) | copy-start | bytes 12582916
  150.6 4.5 %copy-start.8 = (f32[1024,16]{1,0:T(8,128)S(1)}, f32[1024,16]{1,0:T(8,128)}, u32[]{:S(2)}) copy-start(f32[1024,16]{1,0:T(8,128)} %copy-done.7) | copy-start | bytes 196612
  154.3 15.0 %copy-start.18 = (s32[128]{0:T(128)S(1)}, s32[128]{0:T(128)}, u32[]{:S(2)}) copy-start(s32[128]{0:T(128)} %get-tuple-element.31) | copy-start | bytes 1540
  155.1 15.6 %copy-start.13 = (pred[128]{0:T(512)(128)(4,1)S(1)}, pred[128]{0:T(512)(128)(4,1)}, u32[]{:S(2)}) copy-start(pred[128]{0:T(512)(128)(4,1)} %iota_compare_fusion.1) | copy-start | bytes 388
  155.1 15.6 %copy-start.15 = (s32[128]{0:T(128)S(1)}, s32[128]{0:T(128)}, u32[]{:S(2)}) copy-start(s32[128]{0:T(128)} %copy-done.14) | copy-start | bytes 1540
  155.1 15.6 %copy-start.17 = (f32[128]{0:T(128)S(1)}, f32[128]{0:T(128)}, u32[]{:S(2)}) copy-start(f32[128]{0:T(128)} %copy-done.16) | copy-start | bytes 1540
  183.0 84.8 %collective-permute-start.6 = (f32[1,4096]{1,0:T(1,128)}, f32[1,4096]{1,0:T(1,128)S(1)}, u32[]{:S(2)}, u32[]{:S(2)}) collective-permute-start(f32[1,4096]{1,0:T(1,128)} %bitcast.76), channel_id=1, source_target_pairs={{0,2},{2,4},{4,6},{6,8},{8,10},{10,12},{12,14},{14,0},{1,3},{3,5},... | collective-permute-start | bytes 49160 | tf_op jit(solution)/shard_map/ppermute | solution.py:20
  184.4 83.5 %collective-permute-start.5 = (f32[1,4096]{1,0:T(1,128)}, f32[1,4096]{1,0:T(1,128)}, u32[]{:S(2)}, u32[]{:S(2)}) collective-permute-start(f32[1,4096]{1,0:T(1,128)} %bitcast.75), channel_id=1, source_target_pairs={{2,0},{4,2},{6,4},{8,6},{10,8},{12,10},{14,12},{0,14},{3,1},{5,3},... | collective-permute-start | bytes 49160 | tf_op jit(solution)/shard_map/ppermute | solution.py:21
  187.8 80.1 %copy-start.6 = (f32[8,2,8,512]{3,2,0,1:T(8,128)}, f32[8,2,8,512]{3,2,0,1:T(8,128)S(1)}, u32[]{:S(2)}) copy-start(f32[8,2,8,512]{3,2,0,1:T(8,128)S(1)} %copy.162) | copy-start | bytes 786436
  187.9 4.3 %collective-permute-start.8 = (f32[16,64]{1,0:T(8,128)S(1)}, f32[16,64]{1,0:T(8,128)S(1)}, u32[]{:S(2)}, u32[]{:S(2)}) collective-permute-start(f32[16,64]{1,0:T(8,128)S(1)} %get-tuple-element.14), channel_id=1, source_target_pairs={{1,0},{3,2},{5,4},{7,6},{9,8},{11,10},{13,12},{15,14},{17,16},{19,... | collective-permute-start | bytes 12296 | tf_op jit(solution)/shard_map/ppermute | solution.py:21
  189.2 3.8 %collective-permute-start.7 = (f32[16,64]{1,0:T(8,128)S(1)}, f32[16,64]{1,0:T(8,128)S(1)}, u32[]{:S(2)}, u32[]{:S(2)}) collective-permute-start(f32[16,64]{1,0:T(8,128)S(1)} %get-tuple-element.15), channel_id=1, source_target_pairs={{0,1},{2,3},{4,5},{6,7},{8,9},{10,11},{12,13},{14,15},{16,17},{18,... | collective-permute-start | bytes 12296 | tf_op jit(solution)/shard_map/ppermute | solution.py:20
  262.8 5.1 %copy-start.5 = (f32[16,4096]{1,0:T(8,128)S(1)}, f32[16,4096]{1,0:T(8,128)}, u32[]{:S(2)}) copy-start(f32[16,4096]{1,0:T(8,128)} %param.10) | copy-start | bytes 786436
  262.8 5.1 %copy-start.11 = (f32[1,4096]{1,0:T(1,128)S(1)}, f32[1,4096]{1,0:T(1,128)}, u32[]{:S(2)}) copy-start(f32[1,4096]{1,0:T(1,128)} %copy-done.10) | copy-start | bytes 49156

commit v2 on v1

--- a/solution.py
+++ b/solution.py
@@ -3,6 +3,8 @@
 import jax
 import jax.numpy as jnp
 from jax import lax
+from jax.experimental import pallas as pl
+from jax.experimental.pallas import tpu as pltpu
 from jax.sharding import PartitionSpec as P
 
 PLANES = 128
@@ -42,13 +44,70 @@
     return (2.0 * jnp.sin(wave_num * (math.pi / PLANES))) ** 2
 
 
-def stencil(field, span_vel, flux_weight, near_local):
+LANES = 128
+
+
+def padded_rows(block):
+    short = -block.shape[0] % 8
+    if short == 0:
+        return block
+    return jnp.concatenate([block, jnp.zeros((short, block.shape[1]), block.dtype)], axis=0)
+
+
+def flux_of(left, here, right, near, weight):
+    rows = here.shape[0]
+    turned = [pltpu.roll(padded_rows(piece), HALO, 1) for piece in (left, here, right)]
+    full = turned[1].shape
+    lane = lax.broadcasted_iota(jnp.int32, full, 1)
+    low_part = jnp.where(lane < HALO, turned[0], turned[1])
+    high_part = jnp.where(lane < HALO, turned[1], turned[2])
+    total = jnp.zeros_like(here)
+    for slot in range(near.shape[0]):
+        index = jnp.broadcast_to(near[slot : slot + 1], full)
+        within = index & (LANES - 1)
+        low = jnp.take_along_axis(low_part, within, axis=1)
+        high = jnp.take_along_axis(high_part, within, axis=1)
+        picked = jnp.where(index < LANES, low, high)[:rows]
+        total = total + weight[slot : slot + 1] * (picked - here)
+    return total
+
+
+def plane_difference(here, before, after):
+    rows = here.shape[0]
+    full = padded_rows(here)
+    row = lax.broadcasted_iota(jnp.int32, full.shape, 0)
+    ahead = jnp.where(row == rows - 1, after, pltpu.roll(full, full.shape[0] - 1, 0))
+    behind = jnp.where(row == 0, before, pltpu.roll(full, 1, 0))
+    return (ahead - behind)[:rows]
+
+
+def stencil_kernel(start_ref, wide_ref, edge_ref, scalar_ref, vel_ref, weight_ref, near_ref, out_ref):
+    start = start_ref[0]
+
+    @pl.loop(0, out_ref.shape[1] // LANES)
+    def _(block):
+        at = pl.ds(pl.multiple_of(block * LANES, LANES), LANES)
+        left, here, right = (
+            wide_ref[:, pl.ds(pl.multiple_of((block + i) * LANES, LANES), LANES)] for i in range(3)
+        )
+        near = near_ref[:, at] - (start + block * LANES - HALO)
+        flux = flux_of(left, here, right, near, weight_ref[:, at])
+        change = plane_difference(here, edge_ref[0:1, at], edge_ref[1:2, at])
+        out_ref[:, at] = scalar_ref[:, at] - (vel_ref[:, at] * 0.5 * change + flux)
+
+
+def stepped(scalar, field, span_vel, flux_weight, neighbours, start):
     planes_ext = extended(field, (("span", 0),), 1, True)
-    convected = span_vel * 0.5 * (planes_ext[2:] - planes_ext[:-2])
-    widened = extended(field, (("dom", 1),), HALO, False)
-    for slot in range(flux_weight.shape[0]):
-        convected = convected + flux_weight[slot] * (widened[:, near_local[slot]] - field)
-    return convected
+    edge = jnp.concatenate([planes_ext[:1], planes_ext[-1:]], axis=0)
+    wide = extended(field, (("dom", 1),), LANES, False)
+    vmem = pl.BlockSpec(memory_space=pltpu.VMEM)
+    return pl.pallas_call(
+        stencil_kernel,
+        out_shape=jax.ShapeDtypeStruct(field.shape, field.dtype),
+        in_specs=[pl.BlockSpec(memory_space=pltpu.SMEM)] + [vmem] * 6,
+        out_specs=vmem,
+        compiler_params=pltpu.CompilerParams(vmem_limit_bytes=32 * 2**20),
+    )(start.reshape(1), wide, edge, scalar, span_vel, flux_weight, neighbours)
 
 
 def apply_table(table, block):
@@ -73,8 +132,7 @@
     span_pos = lax.axis_index("span")
     cols_count = cell_count // span_count
     cell_start = lax.axis_index("dom") * cell_count
-    near_local = neighbours - cell_start + HALO
-    source = scalar - stencil(scalar, span_vel, flux_weight, near_local)
+    source = stepped(scalar, scalar, span_vel, flux_weight, neighbours, cell_start)
     all_waves = jnp.arange(PLANES, dtype=jnp.int32)
     local_iface = interface - cell_start
     wave_table = fourier_entry(all_waves[:, None], all_waves[None, :])
@@ -126,7 +184,7 @@
     corrected_cols = interior_cols.at[:, slot_cell].add(-back_slots, mode="drop")
     pressure_cols = jnp.dot(wave_table.T, corrected_cols, precision=lax.Precision.HIGHEST)
     pressure = lax.all_to_all(pressure_cols, "span", split_axis=0, concat_axis=1, tiled=True)
-    corrected = scalar - stencil(pressure, span_vel, flux_weight, near_local)
+    corrected = stepped(scalar, pressure, span_vel, flux_weight, neighbours, cell_start)
     return (pressure, corrected)
 
 

time: 271 us -> 136 us (0.50)
  local copies, waits for them, and re-layouts: 172 us -> 24.4 us
  Pallas kernels: 0 us -> 12 us
  waiting for transfers between devices: 11.2 us -> 18 us
  starting transfers between devices: 29 us -> 22.9 us
    gather x16 -> x0, local copies, waits for them, and re-layouts: 145 us -> none  [stencil(): widened[:, near_local[slot]] - field]
    pallas_call x0 -> x2, Pallas kernels: none -> 12 us  [stepped(): pl.pallas_call(stencil_kernel, out_shape=jax.ShapeDtypeStruct(field.shape...]
    concatenate x4 -> x0, local copies, waits for them, and re-layouts: 5.33 us -> none  [extended(): value = jnp.concatenate([before, value, after], axis=dim)]
    ppermute x4, waiting for transfers between devices: 0.81 us -> 4.89 us  [extended(): before = lax.ppermute(last, axis, up)]
    ppermute x4, starting transfers between devices: 12 us -> 7.9 us  [extended(): after = lax.ppermute(initial, axis, down)]
    sub x2 -> x0, other arithmetic: 3.13 us -> none  [the longest x1 1.96 us: on_device(): corrected = scalar - stencil(pressure, span_vel, flux_weight, near_local)]
    unnamed x38 -> x30, local copies, waits for them, and re-layouts: 0.72 us -> 3.63 us
  transfers between devices with their start and end apart: 11 -> 11, of which waited for: 4 -> 5; matrix products, arithmetic and copies ran while one was open for 61% -> 7% of each run, Pallas kernels for 0% -> 0%
where the time goes in v2:
time: 136 us; the launch traced here: 135 us
  matrix products  26.2 us (19%)
  local copies, waits for them, and re-layouts  24.4 us (18%)
  starting transfers between devices  22.9 us (17%)
  blocking collectives  21.1 us (16%)
  waiting for transfers between devices  18 us (13%)
  Pallas kernels  12 us (9%)
  other arithmetic  8.91 us (7%)
    dot_general x3, matrix products, on_device(): jnp.einsum('mnij,mnj->mni', blocks, paired, precision=lax.Precision.HIGHEST)  14.8 us
    pallas_call x2, Pallas kernels, stepped(): pl.pallas_call(stencil_kernel, out_shape=jax.ShapeDtypeStruct(field.shape...  12 us
    all_to_all x1, blocking collectives, on_device(): lax.all_to_all(pressure_cols, 'span', split_axis=0, concat_axis=1, tiled=...  10.9 us
    all_to_all x1, blocking collectives, on_device(): lax.all_to_all(outgoing, 'span', split_axis=1, concat_axis=0, tiled=True)  10.2 us
    ppermute x4, starting transfers between devices, extended(): after = lax.ppermute(initial, axis, down)  7.9 us
    dot_general x3, matrix products, on_device(): jnp.einsum('mnji,mnj->mni', blocks, lowered, precision=lax.Precision.HIGH...  7.33 us
    all_to_all x1, waiting for transfers between devices, on_device(): lax.all_to_all(payload, 'span', split_axis=0, concat_axis=1, tiled=True)  6.9 us
    ppermute x4, starting transfers between devices, extended(): before = lax.ppermute(last, axis, up)  6.04 us
  transfers between devices with their start and end apart: 11, of which 5 were waited for; matrix products, arithmetic and copies ran while one was open for 7% of the time, Pallas kernels for 0%

profile of v2, /device:TPU:0, one launch (start us, length us, event | category | flops | bytes accessed | tf_op | source)
XLA Modules:
  0.0 134.5 jit_solution(4727241466846488320)
XLA Ops:
  1.5 2.3 %collective-permute-start = (f32[16,128]{1,0:T(8,128)S(1)}, f32[16,128]{1,0:T(8,128)S(1)}, u32[]{:S(2)}, u32[]{:S(2)}) collective-permute-start(f32[16,128]{1,0:T(8,128)S(1)} %get-tuple-element.12), channel_id=1, source_target_pairs={{0,1},{2,3},{4,5},{6,7},{8,9},{10,11},{12,13},{14,15},{16,17},{18,... | collective-permute-start | bytes 24584 | tf_op jit(solution)/shard_map/ppermute | solution.py:22
  3.9 1.3 collective-permute-start.1
  6.2 2.4 %collective-permute-start.2 = (f32[1,4096]{1,0:T(1,128)S(1)}, f32[1,4096]{1,0:T(1,128)S(1)}, u32[]{:S(2)}, u32[]{:S(2)}) collective-permute-start(f32[1,4096]{1,0:T(1,128)S(1)} %get-tuple-element.10), channel_id=1, source_target_pairs={{0,2},{2,4},{4,6},{6,8},{8,10},{10,12},{12,14},{14,0},{1,3},{3,5},... | collective-permute-start | bytes 49160 | tf_op jit(solution)/shard_map/ppermute | solution.py:22
  8.6 3.1 %collective-permute-start.3 = (f32[1,4096]{1,0:T(1,128)S(1)}, f32[1,4096]{1,0:T(1,128)S(1)}, u32[]{:S(2)}, u32[]{:S(2)}) collective-permute-start(f32[1,4096]{1,0:T(1,128)S(1)} %get-tuple-element.11), channel_id=1, source_target_pairs={{2,0},{4,2},{6,4},{8,6},{10,8},{12,10},{14,12},{0,14},{3,1},{5,3},... | collective-permute-start | bytes 49160 | tf_op jit(solution)/shard_map/ppermute | solution.py:23
  17.6 5.6 %shard_map.113 = f32[16,4096]{1,0:T(8,128)S(1)} custom-call(s32[1]{0:T(128)} %bitcast.start_ref, f32[16,4352]{1,0:T(8,128)S(1)} %pad_maximum_fusion.wide_ref, f32[2,4096]{1,0:T(2,128)S(1)} %pad_maximum_fusion.2.edge_ref, f32[16,4096]{1,0:T(8,128)S(1)} %copy-done.1, f32[16,4096]{1,0:T(8,128)S(1)} %copy-done.3, f32[4,4096]{1,0:T(4,128)S(1)} %copy-done.5, ...), custom_call_target="tpu_custom_call" | custom-call | tf_op jit(solution)/shard_map/pallas_call | solution.py:104
  24.0 5.4 %all-to-all-start = ((f32[16,8,512]{2,0,1:T(8,128)}), f32[16,8,512]{2,0,1:T(8,128)S(1)}, u32[]{:S(2)}, u32[]{:S(2)}) async-start(f32[16,8,512]{2,0,1:T(8,128)} %bitcast.125), calls=%async_computation | async-start | bytes 524288 | tf_op jit(solution)/shard_map/all_to_all | solution.py:142
  30.2 4.3 %scatter_custom_fusion = s32[128]{0:T(128)S(1)} fusion(s32[1024]{0:T(1024)S(1)} %bitcast.167, s32[1024]{0:T(1024)S(1)} %get-tuple-element.4, s32[]{:T(128)} %constant.60.clone.1), kind=kCustom, calls=%fused_computation.69 | custom fusion | bytes 516 | tf_op jit(solution)/shard_map/scatter | solution.py:156
  35.1 3.5 %all-to-all-done = f32[16,8,512]{2,0,1:T(8,128)S(1)} async-done(((f32[16,8,512]{2,0,1:T(8,128)}), f32[16,8,512]{2,0,1:T(8,128)S(1)}, u32[]{:S(2)}, u32[]{:S(2)}) %all-to-all-start) | async-done | bytes 262176 | tf_op jit(solution)/shard_map/all_to_all | solution.py:142
  40.8 3.6 %all-to-all-start.1 = ((f32[8,16,128]{2,1,0:T(8,128)}), f32[8,16,128]{2,1,0:T(8,128)S(1)}, u32[]{:S(2)}, u32[]{:S(2)}) async-start(f32[8,16,128]{2,1,0:T(8,128)} %bitcast.10), calls=%async_computation.1 | async-start | bytes 131072 | tf_op jit(solution)/shard_map/all_to_all | solution.py:159
  44.4 6.9 %all-to-all-done.1 = f32[8,16,128]{2,1,0:T(8,128)S(1)} async-done(((f32[8,16,128]{2,1,0:T(8,128)}), f32[8,16,128]{2,1,0:T(8,128)S(1)}, u32[]{:S(2)}, u32[]{:S(2)}) %all-to-all-start.1) | async-done | bytes 65568 | tf_op jit(solution)/shard_map/all_to_all | solution.py:159
  51.5 4.0 %gather_fusion.1 = f32[1024,16]{1,0:T(8,128)} fusion(f32[16,1024]{0,1:T(8,128)S(1)} %bitcast.130, s32[1024]{0:T(1024)S(1)} %broadcast_clamp_fusion), kind=kCustom, calls=%fused_computation.1 | custom fusion | bytes 135168 | tf_op jit(solution)/shard_map/gather | solution.py:160
  55.5 1.8 %add_bitcast_fusion = f32[16,4,128,1]{0,2,1,3:T(8,128)} fusion(f32[16,8,128]{0,2,1:T(8,128)} %bitcast.129), kind=kLoop, calls=%fused_computation.24 | loop fusion | flops 8192 | bytes 98304 | tf_op jit(solution)/shard_map/add | solution.py:166
  57.3 1.0 copy.41
  58.4 8.4 %fusion.39 = f32[16,4,1,128]{3,2,1,0:T(1,128)S(1)} fusion(f32[16,4,128,1]{2,3,1,0:T(1,128)S(1)} %copy.41, f32[16,4,128,128]{3,2,1,0:T(8,128)} %param.16), kind=kOutput, calls=%fused_computation.83 | convolution fusion | flops 12582912 | bytes 4259840 | tf_op jit(solution)/shard_map/mnij,mnj->mni/dot_general | solution.py:167
  67.0 3.4 %fusion.40 = f32[16,2,1,128]{3,2,1,0:T(1,128)S(1)} fusion(f32[16,2,128,1]{2,3,1,0:T(1,128)S(1)} %bitcast.153, f32[16,2,128,128]{3,2,1,0:T(8,128)S(1)} %copy-done), kind=kOutput, calls=%fused_computation.84 | convolution fusion | flops 6291456 | bytes 2129920 | tf_op jit(solution)/shard_map/mnij,mnj->mni/dot_general | solution.py:167
  70.3 3.0 %fusion.6 = f32[16,1,128]{2,1,0:T(1,128)S(1)} fusion(f32[16,1,128,128]{3,2,1,0:T(8,128)} %param.18, f32[16,2,128]{2,1,0:T(2,128)S(1)} %bitcast.146), kind=kOutput, calls=%fused_computation.15 | convolution fusion | flops 3147776 | bytes 1073152 | tf_op jit(solution)/shard_map/mnij,mnj->mni/dot_general | solution.py:167
  73.3 1.2 collective-permute-done.4
  74.5 1.7 %convolution_bitcast_fusion = f32[16,128,1]{1,2,0:T(1,128)S(1)} fusion(f32[16,128,1]{1,2,0:T(1,128)S(1)} %bitcast.160, f32[16,1,128,128]{3,2,1,0:T(8,128)S(1)} %copy-done.10), kind=kOutput, calls=%fused_computation.9 | convolution fusion | flops 3145728 | bytes 1064960 | tf_op jit(solution)/shard_map/mnij,mnj->mni/dot_general | solution.py:170
  78.2 1.9 %fusion.41 = f32[16,2,1,128]{3,2,1,0:T(1,128)S(1)} fusion(f32[16,2,128,1]{2,3,1,0:T(1,128)S(1)} %bitcast.155, f32[16,2,128,128]{3,2,1,0:T(8,128)S(1)} %copy-done), kind=kOutput, calls=%fused_computation.85 | convolution fusion | flops 6291456 | bytes 2129920 | tf_op jit(solution)/shard_map/mnji,mnj->mni/dot_general | solution.py:176
  80.9 4.5 %fusion.42 = f32[16,4,1,128]{3,2,1,0:T(1,128)} fusion(f32[16,4,128,1]{2,3,1,0:T(1,128)S(1)} %bitcast.148, f32[16,4,128,128]{3,2,1,0:T(8,128)S(1)} %copy-done.9), kind=kOutput, calls=%fused_computation.86 | convolution fusion | flops 12582912 | bytes 4259840 | tf_op jit(solution)/shard_map/mnji,mnj->mni/dot_general | solution.py:176
  85.4 1.7 %copy.56 = f32[16,4,1,128]{0,3,1,2:T(8,128)} copy(f32[16,4,1,128]{3,2,1,0:T(1,128)} %fusion.42) | data formatting | bytes 65536 | tf_op jit(solution)/shard_map/mnji,mnj->mni/dot_general | solution.py:176
  87.1 1.8 %fusion.10 = f32[16,1024]{0,1:T(8,128)} fusion(f32[1024,16]{1,0:T(8,128)S(1)} %copy-done.12, f32[16,4,128]{0,2,1:T(8,128)} %bitcast.137), kind=kLoop, calls=%fused_computation.20 | loop fusion | flops 32768 | bytes 163840 | tf_op jit(solution)/shard_map/mul | solution.py:181
  88.8 3.6 %scatter_custom_fusion.1 = f32[16,1024]{0,1:T(8,128)S(1)} fusion(s32[1024]{0:T(1024)S(1)} %bitcast.164, f32[16,1024]{0,1:T(8,128)} %fusion.10, f32[]{:T(128)} %constant.67.clone.1), kind=kCustom, calls=%fused_computation.17 | custom fusion | bytes 131076 | tf_op jit(solution)/shard_map/scatter | solution.py:181
  93.3 10.2 %all_to_all.66 = f32[16,8,128]{2,0,1:T(8,128)S(1)} all-to-all(f32[16,8,128]{2,0,1:T(8,128)} %copy.37), channel_id=1, replica_groups=mesh['case'=2,'span'=8,'dom'=2] {'span'}, dimensions={1} | all-to-all | bytes 131072 | tf_op jit(solution)/shard_map/all_to_all | solution.py:183
  103.6 1.5 %scatter_fusion = f32[128,512]{0,1:T(8,128)S(1)} fusion(f32[128,512]{0,1:T(8,128)S(1)} %copy.38, s32[128]{0:T(128)} %get-tuple-element.15, f32[128,128]{1,0:T(8,128)S(1)} %copy.39), kind=kCustom, calls=%fused_computation.4 | custom fusion | flops 16384 | bytes 197120 | tf_op jit(solution)/shard_map/scatter-add | solution.py:184
  105.8 10.9 %all_to_all.67 = f32[8,16,512]{2,1,0:T(8,128)S(1)} all-to-all(f32[8,16,512]{2,1,0:T(8,128)S(1)} %bitcast.138), channel_id=1, replica_groups=mesh['case'=2,'span'=8,'dom'=2] {'span'}, dimensions={0} | all-to-all | bytes 524288 | tf_op jit(solution)/shard_map/all_to_all | solution.py:186
  116.8 1.3 collective-permute-start.5
  118.1 1.3 collective-permute-start.6
  119.4 2.2 %collective-permute-start.8 = (f32[1,4096]{1,0:T(1,128)S(1)}, f32[1,4096]{1,0:T(1,128)S(1)}, u32[]{:S(2)}, u32[]{:S(2)}) collective-permute-start(f32[1,4096]{1,0:T(1,128)S(1)} %bitcast.166), channel_id=1, source_target_pairs={{2,0},{4,2},{6,4},{8,6},{10,8},{12,10},{14,12},{0,14},{3,1},{5,3},... | collective-permute-start | bytes 49160 | tf_op jit(solution)/shard_map/ppermute | solution.py:23
  121.7 1.6 %collective-permute-done.8 = f32[1,4096]{1,0:T(1,128)S(1)} collective-permute-done((f32[1,4096]{1,0:T(1,128)S(1)}, f32[1,4096]{1,0:T(1,128)S(1)}, u32[]{:S(2)}, u32[]{:S(2)}) %collective-permute-start.8) | collective-permute-done | bytes 16416 | tf_op jit(solution)/shard_map/ppermute | solution.py:23
  123.2 4.9 %collective-permute-done.7 = f32[1,4096]{1,0:T(1,128)S(1)} collective-permute-done((f32[1,4096]{1,0:T(1,128)S(1)}, f32[1,4096]{1,0:T(1,128)S(1)}, u32[]{:S(2)}, u32[]{:S(2)}) %collective-permute-start.7) | collective-permute-done | bytes 16416 | tf_op jit(solution)/shard_map/ppermute | solution.py:22
  128.2 6.3 %shard_map.114 = f32[16,4096]{1,0:T(8,128)} custom-call(s32[1]{0:T(128)} %bitcast.start_ref, f32[16,4352]{1,0:T(8,128)S(1)} %pad_maximum_fusion.1.wide_ref, f32[2,4096]{1,0:T(2,128)S(1)} %pad_maximum_fusion.3.edge_ref, f32[16,4096]{1,0:T(8,128)S(1)} %copy-done.2, f32[16,4096]{1,0:T(8,128)S(1)} %copy-done.4, f32[4,4096]{1,0:T(4,128)S(1)} %copy-done.6, ...), custom_call_target="tpu_custom_call" | custom-call | tf_op jit(solution)/shard_map/pallas_call | solution.py:104
  (79 shorter events, 16.9 us)
Async XLA Ops:
  0.6 66.3 %copy-start = (f32[16,2,128,128]{3,2,1,0:T(8,128)S(1)}, f32[16,2,128,128]{3,2,1,0:T(8,128)}, u32[]{:S(2)}) copy-start(f32[16,2,128,128]{3,2,1,0:T(8,128)} %param.17) | copy-start | bytes 6291460
  1.5 11.5 %collective-permute-start = (f32[16,128]{1,0:T(8,128)S(1)}, f32[16,128]{1,0:T(8,128)S(1)}, u32[]{:S(2)}, u32[]{:S(2)}) collective-permute-start(f32[16,128]{1,0:T(8,128)S(1)} %get-tuple-element.12), channel_id=1, source_target_pairs={{0,1},{2,3},{4,5},{6,7},{8,9},{10,11},{12,13},{14,15},{16,17},{18,... | collective-permute-start | bytes 24584 | tf_op jit(solution)/shard_map/ppermute | solution.py:22
  3.9 9.1 %collective-permute-start.1 = (f32[16,128]{1,0:T(8,128)S(1)}, f32[16,128]{1,0:T(8,128)S(1)}, u32[]{:S(2)}, u32[]{:S(2)}) collective-permute-start(f32[16,128]{1,0:T(8,128)S(1)} %get-tuple-element.13), channel_id=1, source_target_pairs={{1,0},{3,2},{5,4},{7,6},{9,8},{11,10},{13,12},{15,14},{17,16},{19,... | collective-permute-start | bytes 24584 | tf_op jit(solution)/shard_map/ppermute | solution.py:23
  6.2 7.8 %collective-permute-start.2 = (f32[1,4096]{1,0:T(1,128)S(1)}, f32[1,4096]{1,0:T(1,128)S(1)}, u32[]{:S(2)}, u32[]{:S(2)}) collective-permute-start(f32[1,4096]{1,0:T(1,128)S(1)} %get-tuple-element.10), channel_id=1, source_target_pairs={{0,2},{2,4},{4,6},{6,8},{8,10},{10,12},{12,14},{14,0},{1,3},{3,5},... | collective-permute-start | bytes 49160 | tf_op jit(solution)/shard_map/ppermute | solution.py:22
  8.6 5.4 %collective-permute-start.3 = (f32[1,4096]{1,0:T(1,128)S(1)}, f32[1,4096]{1,0:T(1,128)S(1)}, u32[]{:S(2)}, u32[]{:S(2)}) collective-permute-start(f32[1,4096]{1,0:T(1,128)S(1)} %get-tuple-element.11), channel_id=1, source_target_pairs={{2,0},{4,2},{6,4},{8,6},{10,8},{12,10},{14,12},{0,14},{3,1},{5,3},... | collective-permute-start | bytes 49160 | tf_op jit(solution)/shard_map/ppermute | solution.py:23
  14.0 1.0 copy-start.1
  15.0 0.9 copy-start.3
  15.9 0.8 copy-start.5
  16.8 0.8 copy-start.7
  24.0 14.6 %all-to-all-start = ((f32[16,8,512]{2,0,1:T(8,128)}), f32[16,8,512]{2,0,1:T(8,128)S(1)}, u32[]{:S(2)}, u32[]{:S(2)}) async-start(f32[16,8,512]{2,0,1:T(8,128)} %bitcast.125), calls=%async_computation | async-start | bytes 524288 | tf_op jit(solution)/shard_map/all_to_all | solution.py:142
  40.8 10.5 %all-to-all-start.1 = ((f32[8,16,128]{2,1,0:T(8,128)}), f32[8,16,128]{2,1,0:T(8,128)S(1)}, u32[]{:S(2)}, u32[]{:S(2)}) async-start(f32[8,16,128]{2,1,0:T(8,128)} %bitcast.10), calls=%async_computation.1 | async-start | bytes 131072 | tf_op jit(solution)/shard_map/all_to_all | solution.py:159
  55.5 19.0 %copy-start.10 = (f32[16,1,128,128]{3,2,1,0:T(8,128)S(1)}, f32[16,1,128,128]{3,2,1,0:T(8,128)}, u32[]{:S(2)}) copy-start(f32[16,1,128,128]{3,2,1,0:T(8,128)} %param.19) | copy-start | bytes 3145732
  66.8 9.4 %copy-start.14 = (f32[16,4,1,128]{3,2,1,0:T(1,128)}, f32[16,4,1,128]{3,2,1,0:T(1,128)S(1)}, u32[]{:S(2)}) copy-start(f32[16,4,1,128]{3,2,1,0:T(1,128)S(1)} %fusion.39) | copy-start | bytes 98308
  66.9 10.3 %copy-start.11 = (f32[16,1,128,128]{3,2,1,0:T(8,128)S(1)}, f32[16,1,128,128]{3,2,1,0:T(8,128)}, u32[]{:S(2)}) copy-start(f32[16,1,128,128]{3,2,1,0:T(8,128)} %param.18) | copy-start | bytes 3145732
  67.0 13.9 %copy-start.9 = (f32[16,4,128,128]{3,2,1,0:T(8,128)S(1)}, f32[16,4,128,128]{3,2,1,0:T(8,128)}, u32[]{:S(2)}) copy-start(f32[16,4,128,128]{3,2,1,0:T(8,128)} %param.16) | copy-start | bytes 12582916
  73.3 1.2 collective-permute-start.4
  77.2 9.8 %copy-start.12 = (f32[1024,16]{1,0:T(8,128)S(1)}, f32[1024,16]{1,0:T(8,128)}, u32[]{:S(2)}) copy-start(f32[1024,16]{1,0:T(8,128)} %gather_fusion.1) | copy-start | bytes 196612
  85.4 42.8 %copy-start.2 = (f32[16,4096]{1,0:T(8,128)S(1)}, f32[16,4096]{1,0:T(8,128)}, u32[]{:S(2)}) copy-start(f32[16,4096]{1,0:T(8,128)} %scalar_ref.3) | copy-start | bytes 786436
  85.4 42.8 %copy-start.4 = (f32[16,4096]{1,0:T(8,128)S(1)}, f32[16,4096]{1,0:T(8,128)}, u32[]{:S(2)}) copy-start(f32[16,4096]{1,0:T(8,128)} %vel_ref.3) | copy-start | bytes 786436
  85.4 42.8 %copy-start.6 = (f32[4,4096]{1,0:T(4,128)S(1)}, f32[4,4096]{1,0:T(4,128)}, u32[]{:S(2)}) copy-start(f32[4,4096]{1,0:T(4,128)} %weight_ref.3) | copy-start | bytes 196612
  85.4 42.8 %copy-start.8 = (s32[4,4096]{1,0:T(4,128)S(1)}, s32[4,4096]{1,0:T(4,128)}, u32[]{:S(2)}) copy-start(s32[4,4096]{1,0:T(4,128)} %near_ref.3) | copy-start | bytes 196612
  116.8 17.8 %copy-start.13 = (f32[8,2,8,512]{3,2,0,1:T(8,128)}, f32[8,2,8,512]{3,2,0,1:T(8,128)S(1)}, u32[]{:S(2)}) copy-start(f32[8,2,8,512]{3,2,0,1:T(8,128)S(1)} %copy.58) | copy-start | bytes 786436
  116.8 4.8 %collective-permute-start.5 = (f32[16,128]{1,0:T(8,128)S(1)}, f32[16,128]{1,0:T(8,128)S(1)}, u32[]{:S(2)}, u32[]{:S(2)}) collective-permute-start(f32[16,128]{1,0:T(8,128)S(1)} %get-tuple-element.8), channel_id=1, source_target_pairs={{0,1},{2,3},{4,5},{6,7},{8,9},{10,11},{12,13},{14,15},{16,17},{18,... | collective-permute-start | bytes 24584 | tf_op jit(solution)/shard_map/ppermute | solution.py:22
  118.1 3.6 %collective-permute-start.6 = (f32[16,128]{1,0:T(8,128)S(1)}, f32[16,128]{1,0:T(8,128)S(1)}, u32[]{:S(2)}, u32[]{:S(2)}) collective-permute-start(f32[16,128]{1,0:T(8,128)S(1)} %get-tuple-element.9), channel_id=1, source_target_pairs={{1,0},{3,2},{5,4},{7,6},{9,8},{11,10},{13,12},{15,14},{17,16},{19,... | collective-permute-start | bytes 24584 | tf_op jit(solution)/shard_map/ppermute | solution.py:23
  119.4 3.8 %collective-permute-start.8 = (f32[1,4096]{1,0:T(1,128)S(1)}, f32[1,4096]{1,0:T(1,128)S(1)}, u32[]{:S(2)}, u32[]{:S(2)}) collective-permute-start(f32[1,4096]{1,0:T(1,128)S(1)} %bitcast.166), channel_id=1, source_target_pairs={{2,0},{4,2},{6,4},{8,6},{10,8},{12,10},{14,12},{0,14},{3,1},{5,3},... | collective-permute-start | bytes 49160 | tf_op jit(solution)/shard_map/ppermute | solution.py:23
  121.6 6.5 %collective-permute-start.7 = (f32[1,4096]{1,0:T(1,128)S(1)}, f32[1,4096]{1,0:T(1,128)S(1)}, u32[]{:S(2)}, u32[]{:S(2)}) collective-permute-start(f32[1,4096]{1,0:T(1,128)S(1)} %bitcast.165), channel_id=1, source_target_pairs={{0,2},{2,4},{4,6},{6,8},{8,10},{10,12},{12,14},{14,0},{1,3},{3,5},... | collective-permute-start | bytes 49160 | tf_op jit(solution)/shard_map/ppermute | solution.py:22

commit v3 on v2

--- a/solution.py
+++ b/solution.py
@@ -1,3 +1,4 @@
+import functools
 import math
 
 import jax
@@ -23,10 +24,6 @@
         after = lax.ppermute(initial, axis, down)
         value = jnp.concatenate([before, value, after], axis=dim)
     return value
-
-
-def swapped(value, axis, distance):
-    return lax.ppermute(value, axis, [(i, i ^ 1 << distance) for i in range(lax.axis_size(axis))])
 
 
 def fourier_entry(wave_ids, plane_ids):
@@ -110,8 +107,186 @@
     )(start.reshape(1), wide, edge, scalar, span_vel, flux_weight, neighbours)
 
 
-def apply_table(table, block):
-    return jnp.einsum("rp,pxc->rxc", table, block, precision=lax.Precision.HIGHEST)
+def exact_dot(left, right, dims):
+    return lax.dot_general(
+        left, right, (dims, ((), ())), precision=lax.Precision.HIGHEST, preferred_element_type=jnp.float32
+    )
+
+
+def row_product(row, matrix, dim):
+    rows = jnp.broadcast_to(row, (8, row.shape[1]))
+    high = rows.astype(jnp.bfloat16).astype(jnp.float32)
+    both = jnp.concatenate([high, rows - high], axis=0).astype(jnp.bfloat16)
+    coarse = matrix.astype(jnp.bfloat16)
+    fine = (matrix - coarse.astype(jnp.float32)).astype(jnp.bfloat16)
+    dims = (((1,), (dim,)), ((), ()))
+    main = lax.dot_general(both, coarse, dims, preferred_element_type=jnp.float32)
+    rest = lax.dot_general(both, fine, dims, preferred_element_type=jnp.float32)
+    return main[0:1] + (main[8:9] + (rest[0:1] + rest[8:9]))
+
+
+def climb(below, blocks, above):
+    @pl.loop(0, blocks.shape[0], unroll=4)
+    def _(wave):
+        at = pl.ds(wave, 1)
+        for node in range(blocks.shape[1]):
+            pair = below[2 * node, at, :] + below[2 * node + 1, at, :]
+            above[node, at, :] = row_product(pair, blocks[wave, node], 1)
+
+
+def descend(below, blocks, lowered, result):
+    @pl.loop(0, blocks.shape[0], unroll=4)
+    def _(wave):
+        at = pl.ds(wave, 1)
+        for node in range(blocks.shape[1]):
+            returned = row_product(lowered[node, at, :], blocks[wave, node], 0)
+            for child in (2 * node, 2 * node + 1):
+                result[child, at, :] = below[child, at, :] - returned
+
+
+def spectral_kernel(
+    span_count, source_ref, table_ref, diag_ref, shift_ref, iface_ref, one_hbm, two_hbm, three_hbm, root_hbm, out_ref,
+    one, two, three, root, source_in, leaf_out, leaf_in, press_out, press_in, back_in, fix_out, fix_in,
+    s0, s1, s2, s3, g0, g1, g2, g3, partner, load_sem, send_sem, recv_sem, swap_sem,
+):
+    planes, cells = source_ref.shape
+    cols = cells // span_count
+    domains, slots = iface_ref.shape
+    shares = span_count // domains
+    me = lax.axis_index("span")
+    half = lax.axis_index("dom")
+    barrier = pltpu.get_barrier_semaphore()
+    kind = pl.DeviceIdType.MESH
+    loads = [
+        pltpu.make_async_copy(src, dst, load_sem.at[i])
+        for i, (src, dst) in enumerate(((one_hbm, one), (two_hbm, two), (three_hbm, three), (root_hbm, root)))
+    ]
+    for load in loads:
+        load.start()
+    peers = [lax.rem(me + i, span_count) for i in range(1, span_count)]
+    for peer in peers:
+        pl.semaphore_signal(barrier, inc=1, device_id={"span": peer}, device_id_type=kind)
+    pl.semaphore_signal(barrier, inc=1, device_id={"dom": 1 - half}, device_id_type=kind)
+    pl.semaphore_wait(barrier, span_count)
+
+    def exchange(phase, pick, landing):
+        copies = []
+        for i, peer in enumerate(peers):
+            copies.append(
+                pltpu.make_async_remote_copy(
+                    src_ref=pick(peer),
+                    dst_ref=landing.at[me],
+                    send_sem=send_sem.at[phase, i],
+                    recv_sem=recv_sem.at[phase, i],
+                    device_id={"span": peer},
+                    device_id_type=kind,
+                )
+            )
+            copies[-1].start()
+        return copies
+
+    def arrived(copies):
+        for copy in copies:
+            copy.wait_recv()
+
+    def columns_of(owner):
+        return pl.ds(pl.multiple_of(owner * cols, LANES), cols)
+
+    def hot(domain_row, first):
+        cell = lax.broadcasted_iota(jnp.int32, (cols, slots), 0) + first
+        return (cell == domain_row).astype(jnp.float32)
+
+    sent = exchange(0, lambda peer: source_ref.at[:, columns_of(peer)], source_in)
+    source_in[me] = source_ref[:, columns_of(me)]
+    own_domain = lax.div(me, shares)
+    own_hot = hot(iface_ref[pl.ds(own_domain, 1), :], half * cells + me * cols)
+    divisor = diag_ref[:, columns_of(me)] + shift_ref[...]
+    arrived(sent)
+    block = source_in[...].reshape(span_count * planes, cols)
+    interior = exact_dot(table_ref[...], block, ((1,), (0,))) / divisor
+    leaf_out[...] = exact_dot(interior, own_hot, ((1,), (0,))).reshape(leaf_out.shape)
+    leaves = exchange(1, lambda peer: leaf_out.at[peer], leaf_in)
+    leaf_in[me] = leaf_out[me]
+    press_out[...] = exact_dot(table_ref[...], interior, ((0,), (0,))).reshape(press_out.shape)
+    for load in loads:
+        load.wait()
+    arrived(leaves)
+    pressed = exchange(2, lambda peer: press_out.at[peer], press_in)
+    press_in[me] = press_out[me]
+    for domain in range(domains):
+        s0[domain] = sum(leaf_in[domain * shares + i] for i in range(shares))
+    climb(s0, one, s1)
+    climb(s1, two, s2)
+    climb(s2, three, s3)
+    swap = pltpu.make_async_remote_copy(
+        src_ref=s3,
+        dst_ref=partner,
+        send_sem=swap_sem.at[0],
+        recv_sem=swap_sem.at[1],
+        device_id={"dom": 1 - half},
+        device_id_type=kind,
+    )
+    swap.start()
+    swap.wait_recv()
+
+    @pl.loop(0, planes, unroll=4)
+    def _(wave):
+        at = pl.ds(wave, 1)
+        top = row_product(s3[0, at, :] + partner[0, at, :], root[wave, 0], 1)
+        g3[0, at, :] = s3[0, at, :] - row_product(top, root[wave, 0], 0)
+
+    descend(s2, three, g3, g2)
+    descend(s1, two, g2, g1)
+    descend(s0, one, g1, g0)
+    backs = exchange(3, lambda peer: g0.at[lax.div(peer, shares)], back_in)
+    back_in[me] = g0[own_domain]
+    arrived(backs)
+    back = back_in[...].reshape(span_count * planes, slots)
+    fix_out[...] = exact_dot(table_ref[...], 0.5 * back, ((0,), (0,))).reshape(fix_out.shape)
+    fixes = exchange(4, lambda peer: fix_out.at[peer], fix_in)
+    fix_in[me] = fix_out[me]
+    arrived(pressed)
+    arrived(fixes)
+
+    @pl.loop(0, span_count)
+    def _(owner):
+        domain = lax.div(owner, shares)
+        where = hot(iface_ref[pl.ds(domain, 1), :], half * cells + owner * cols)
+        added = exact_dot(fix_in[domain * shares], where, ((1,), (1,)))
+        out_ref[:, columns_of(owner)] = press_in[owner] - added
+
+    for copies in (sent, leaves, pressed, backs, fixes, [swap]):
+        for copy in copies:
+            copy.wait_send()
+
+
+def projected(source, table, diagonal, shift, interface, blocks, span_count):
+    planes, cells = source.shape
+    cols = cells // span_count
+    domains, slots = interface.shape
+    vmem = pl.BlockSpec(memory_space=pltpu.VMEM)
+    hbm = pl.BlockSpec(memory_space=pl.ANY)
+    wide, narrow = (span_count, planes, cols), (span_count, planes, slots)
+    nodes = [domains >> level for level in range(4)]
+    levels = [(node, planes, slots) for node in nodes]
+    shapes = [wide, narrow, narrow, wide, wide, narrow, narrow, narrow] + levels + levels + [levels[3]]
+    return pl.pallas_call(
+        functools.partial(spectral_kernel, span_count),
+        out_shape=jax.ShapeDtypeStruct(source.shape, source.dtype),
+        in_specs=[vmem] * 5 + [hbm] * 4,
+        out_specs=vmem,
+        scratch_shapes=[pltpu.VMEM(block.shape, block.dtype) for block in blocks]
+        + [pltpu.VMEM(shape, jnp.float32) for shape in shapes]
+        + [
+            pltpu.SemaphoreType.DMA((4,)),
+            pltpu.SemaphoreType.DMA((5, span_count - 1)),
+            pltpu.SemaphoreType.DMA((5, span_count - 1)),
+            pltpu.SemaphoreType.DMA((2,)),
+        ],
+        compiler_params=pltpu.CompilerParams(
+            collective_id=0, has_side_effects=True, vmem_limit_bytes=40 * 2**20
+        ),
+    )(source, table, diagonal, shift, interface, *blocks)
 
 
 def on_device(
@@ -126,64 +301,15 @@
     schur_three,
     schur_root,
 ):
-    plane_count = scalar.shape[0]
-    cell_count = scalar.shape[1]
-    span_count = lax.axis_size("span")
-    span_pos = lax.axis_index("span")
-    cols_count = cell_count // span_count
-    cell_start = lax.axis_index("dom") * cell_count
+    cell_start = lax.axis_index("dom") * scalar.shape[1]
+    waves = jnp.arange(PLANES, dtype=jnp.int32)
+    table = fourier_entry(waves[:, None], waves[None, :])
+    shift = wave_shift(waves)[:, None]
     source = stepped(scalar, scalar, span_vel, flux_weight, neighbours, cell_start)
-    all_waves = jnp.arange(PLANES, dtype=jnp.int32)
-    local_iface = interface - cell_start
-    wave_table = fourier_entry(all_waves[:, None], all_waves[None, :])
-    slot_count = min(cols_count, interface.shape[1] * max(1, cols_count // CELL_DOM))
-    grouped = source.reshape(plane_count, span_count, cols_count)
-    spectrum_cols = apply_table(
-        wave_table, lax.all_to_all(grouped, "span", split_axis=1, concat_axis=0, tiled=True)
-    ).reshape(PLANES, cols_count)
-    diag_cols = lax.dynamic_slice_in_dim(diagonal, span_pos * cols_count, cols_count)
-    interior_cols = spectrum_cols / (diag_cols[None, :] + wave_shift(all_waves)[:, None])
-    flat_iface = local_iface.reshape(-1)
-    owner = flat_iface // cols_count
-    order = jnp.arange(flat_iface.shape[0], dtype=jnp.int32)
-    earlier = (owner[:, None] == owner[None, :]) & (order[None, :] < order[:, None])
-    ranks = jnp.sum(earlier.astype(jnp.int32), 1)
-    slot_index = owner * slot_count + ranks
-    owned = owner == span_pos
-    slot_cell = (
-        jnp.full((slot_count,), cols_count, jnp.int32)
-        .at[jnp.where(owned, ranks, slot_count)]
-        .set(flat_iface - span_pos * cols_count, mode="drop")
-    )
-    payload = interior_cols[:, jnp.minimum(slot_cell, cols_count - 1)]
-    received = lax.all_to_all(payload, "span", split_axis=0, concat_axis=1, tiled=True)
-    leaves = received[:, slot_index].reshape(
-        plane_count, local_iface.shape[0], local_iface.shape[1]
-    )
-    levels = [leaves]
-    current = leaves
-    for blocks in (schur_one, schur_two, schur_three):
-        paired = current[:, 0::2] + current[:, 1::2]
-        current = jnp.einsum("mnij,mnj->mni", blocks, paired, precision=lax.Precision.HIGHEST)
-        levels.append(current)
-    partner = swapped(current, "dom", 0)
-    top_value = jnp.einsum(
-        "mnij,mnj->mni", schur_root, current + partner, precision=lax.Precision.HIGHEST
-    )
-    returned = jnp.einsum("mnji,mnj->mni", schur_root, top_value, precision=lax.Precision.HIGHEST)
-    lowered = levels[3] - returned
-    for blocks, below in ((schur_three, levels[2]), (schur_two, levels[1]), (schur_one, levels[0])):
-        returned = jnp.einsum("mnji,mnj->mni", blocks, lowered, precision=lax.Precision.HIGHEST)
-        lowered = below - jnp.repeat(returned, 2, axis=1)
-    outgoing = (
-        jnp.zeros((plane_count, span_count * slot_count), jnp.float32)
-        .at[:, slot_index]
-        .set(0.5 * lowered.reshape(plane_count, -1))
-    )
-    back_slots = lax.all_to_all(outgoing, "span", split_axis=1, concat_axis=0, tiled=True)
-    corrected_cols = interior_cols.at[:, slot_cell].add(-back_slots, mode="drop")
-    pressure_cols = jnp.dot(wave_table.T, corrected_cols, precision=lax.Precision.HIGHEST)
-    pressure = lax.all_to_all(pressure_cols, "span", split_axis=0, concat_axis=1, tiled=True)
+    blocks = (schur_one, schur_two, schur_three, schur_root)
+    pressure = projected(
+        source, table, diagonal[None, :], shift, interface, blocks, lax.axis_size("span")
+    )
     corrected = stepped(scalar, pressure, span_vel, flux_weight, neighbours, cell_start)
     return (pressure, corrected)
 

time: 136 us -> 89.1 us (0.66)
  Pallas kernels: 12 us -> 54 us
  matrix products: 26.2 us -> 0 us
  blocking collectives: 21.1 us -> 0 us
  waiting for transfers between devices: 18 us -> 1.72 us
  local copies, waits for them, and re-layouts: 24.4 us -> 13.8 us
  other arithmetic: 8.91 us -> 1.65 us
  starting transfers between devices: 22.9 us -> 16.5 us
    pallas_call x0 -> x1, Pallas kernels: none -> 42 us  [projected(): pl.pallas_call(functools.partial(spectral_kernel, span_count), out_shape=...]
    dot_general x10 -> x0, matrix products: 26.2 us -> none  [the longest x3 14.8 us: on_device(): jnp.einsum('mnij,mnj->mni', blocks, paired, precision=lax.Precision.HIGHEST)]
    all_to_all x2 -> x0, blocking collectives: 21.1 us -> none  [the longest x1 10.9 us: on_device(): lax.all_to_all(pressure_cols, 'span', split_axis=0, concat_axis=1, tiled=...]
    all_to_all x2 -> x0, waiting for transfers between devices: 10.4 us -> none  [the longest x1 6.9 us: on_device(): lax.all_to_all(payload, 'span', split_axis=0, concat_axis=1, tiled=True)]
    all_to_all x2 -> x0, starting transfers between devices: 9 us -> none  [the longest x1 5.41 us: on_device(): lax.all_to_all(grouped, 'span', split_axis=1, concat_axis=0, tiled=True)]
    unnamed x30 -> x29, local copies, waits for them, and re-layouts: 3.63 us -> 11.9 us
    scatter x2 -> x0, local copies, waits for them, and re-layouts: 7.94 us -> none  [the longest x1 4.3 us: on_device(): slot_cell = jnp.full((slot_count,), cols_count, jnp.int32).at[jnp.where(o...]
    gather x3 -> x0, local copies, waits for them, and re-layouts: 5.39 us -> none  [the longest x1 4.02 us: on_device(): received[:, slot_index]]
  transfers between devices with their start and end apart: 11 -> 8, of which waited for: 5 -> 1; matrix products, arithmetic and copies ran while one was open for 7% -> 3% of each run, Pallas kernels for 0% -> 0%
where the time goes in v3:
time: 89.1 us; the launch traced here: 88.4 us
  Pallas kernels  54 us (61%)
  starting transfers between devices  16.5 us (19%)
  local copies, waits for them, and re-layouts  13.8 us (15%)
  waiting for transfers between devices  1.72 us (2%)
  other arithmetic  1.65 us (2%)
    pallas_call x1, Pallas kernels, projected(): pl.pallas_call(functools.partial(spectral_kernel, span_count), out_shape=...  42 us
    pallas_call x2, Pallas kernels, stepped(): pl.pallas_call(stencil_kernel, out_shape=jax.ShapeDtypeStruct(field.shape...  12 us
    unnamed x29, local copies, waits for them, and re-layouts  11.9 us
    ppermute x4, starting transfers between devices, extended(): after = lax.ppermute(initial, axis, down)  9.71 us
    ppermute x4, starting transfers between devices, extended(): before = lax.ppermute(last, axis, up)  6.79 us
  transfers between devices with their start and end apart: 8, of which 1 were waited for; matrix products, arithmetic and copies ran while one was open for 3% of the time, Pallas kernels for 0%

profile of v3, /device:TPU:0, one launch (start us, length us, event | category | flops | bytes accessed | tf_op | source)
XLA Modules:
  0.0 88.4 jit_solution(15108778385841043785)
XLA Ops:
  0.6 0.7 fusion.11
  1.3 2.3 %collective-permute-start = (f32[16,128]{1,0:T(8,128)S(1)}, f32[16,128]{1,0:T(8,128)S(1)}, u32[]{:S(2)}, u32[]{:S(2)}) collective-permute-start(f32[16,128]{1,0:T(8,128)S(1)} %get-tuple-element.8), channel_id=1, source_target_pairs={{0,1},{2,3},{4,5},{6,7},{8,9},{10,11},{12,13},{14,15},{16,17},{18,... | collective-permute-start | bytes 24584 | tf_op jit(solution)/shard_map/ppermute | solution.py:23
  3.7 1.3 %collective-permute-start.1 = (f32[16,128]{1,0:T(8,128)S(1)}, f32[16,128]{1,0:T(8,128)S(1)}, u32[]{:S(2)}, u32[]{:S(2)}) collective-permute-start(f32[16,128]{1,0:T(8,128)S(1)} %get-tuple-element.9), channel_id=1, source_target_pairs={{1,0},{3,2},{5,4},{7,6},{9,8},{11,10},{13,12},{15,14},{17,16},{19,... | collective-permute-start | bytes 24584 | tf_op jit(solution)/shard_map/ppermute | solution.py:24
  5.0 1.0 %fusion.10 = (f32[1,4096]{1,0:T(1,128)S(1)}, f32[1,4096]{1,0:T(1,128)S(1)}) fusion(f32[16,4096]{1,0:T(8,128)} %scalar_ref.3), kind=kLoop, calls=%fused_computation.23 | loop fusion | bytes 65536 | tf_op jit(solution)/shard_map/slice | solution.py:21
  6.0 2.4 %collective-permute-start.2 = (f32[1,4096]{1,0:T(1,128)S(1)}, f32[1,4096]{1,0:T(1,128)S(1)}, u32[]{:S(2)}, u32[]{:S(2)}) collective-permute-start(f32[1,4096]{1,0:T(1,128)S(1)} %get-tuple-element.6), channel_id=1, source_target_pairs={{0,2},{2,4},{4,6},{6,8},{8,10},{10,12},{12,14},{14,0},{1,3},{3,5},... | collective-permute-start | bytes 49160 | tf_op jit(solution)/shard_map/ppermute | solution.py:23
  8.4 3.1 %collective-permute-start.3 = (f32[1,4096]{1,0:T(1,128)S(1)}, f32[1,4096]{1,0:T(1,128)S(1)}, u32[]{:S(2)}, u32[]{:S(2)}) collective-permute-start(f32[1,4096]{1,0:T(1,128)S(1)} %get-tuple-element.7), channel_id=1, source_target_pairs={{2,0},{4,2},{6,4},{8,6},{10,8},{12,10},{14,12},{0,14},{3,1},{5,3},... | collective-permute-start | bytes 49160 | tf_op jit(solution)/shard_map/ppermute | solution.py:24
  11.5 0.1 copy.13
  11.7 0.2 multiply_multiply_fusion.shift_ref
  11.9 0.3 select_multiply_fusion.table_ref
  12.2 0.0 collective-permute-done
  12.3 1.0 %pad_maximum_fusion.wide_ref = f32[16,4352]{1,0:T(8,128)S(1)} fusion(f32[16,128]{1,0:T(8,128)S(1)} %collective-permute-done.1, f32[16,4096]{1,0:T(8,128)} %scalar_ref.3, f32[16,128]{1,0:T(8,128)S(1)} %collective-permute-done), kind=kLoop, calls=%fused_computation | loop fusion | flops 139264 | bytes 557056 | tf_op jit(solution)/shard_map/concatenate | solution.py:25
  13.3 0.0 copy-start.1
  13.3 0.9 %copy-done.1 = f32[16,4096]{1,0:T(8,128)S(1)} copy-done((f32[16,4096]{1,0:T(8,128)S(1)}, f32[16,4096]{1,0:T(8,128)}, u32[]{:S(2)}) %copy-start.1) | copy-done | bytes 262168
  14.3 0.9 %copy-done.4 = f32[16,4096]{1,0:T(8,128)S(1)} copy-done((f32[16,4096]{1,0:T(8,128)S(1)}, f32[16,4096]{1,0:T(8,128)}, u32[]{:S(2)}) %copy-start.4) | copy-done | bytes 262168
  15.2 0.8 copy-done.8
  16.0 0.8 copy-done.10
  16.9 5.6 %shard_map.113.source_ref = f32[16,4096]{1,0:T(8,128)S(1)} custom-call(s32[1]{0:T(128)} %bitcast.start_ref, f32[16,4352]{1,0:T(8,128)S(1)} %pad_maximum_fusion.wide_ref, f32[2,4096]{1,0:T(2,128)S(1)} %pad_maximum_fusion.2.edge_ref, f32[16,4096]{1,0:T(8,128)S(1)} %copy-done.1, f32[16,4096]{1,0:T(8,128)S(1)} %copy-done.4, f32[4,4096]{1,0:T(4,128)S(1)} %copy-done.8, ...), custom_call_target="tpu_custom_call" | custom-call | tf_op jit(solution)/shard_map/pallas_call | solution.py:101
  22.5 0.0 copy-start
  22.5 2.2 %copy-done = f32[16,4,128,128]{3,2,1,0:T(8,128)S(1)} copy-done((f32[16,4,128,128]{3,2,1,0:T(8,128)S(1)}, f32[16,4,128,128]{3,2,1,0:T(8,128)}, u32[]{:S(2)}) %copy-start) | copy-done | bytes 4194328
  24.7 1.6 %copy-done.3 = f32[16,2,128,128]{3,2,1,0:T(8,128)S(1)} copy-done((f32[16,2,128,128]{3,2,1,0:T(8,128)S(1)}, f32[16,2,128,128]{3,2,1,0:T(8,128)}, u32[]{:S(2)}) %copy-start.3) | copy-done | bytes 2097176
  26.3 1.2 %copy-done.6 = f32[16,1,128,128]{3,2,1,0:T(8,128)S(1)} copy-done((f32[16,1,128,128]{3,2,1,0:T(8,128)S(1)}, f32[16,1,128,128]{3,2,1,0:T(8,128)}, u32[]{:S(2)}) %copy-start.6) | copy-done | bytes 1048600
  27.5 1.2 %copy-done.7 = f32[16,1,128,128]{3,2,1,0:T(8,128)S(1)} copy-done((f32[16,1,128,128]{3,2,1,0:T(8,128)S(1)}, f32[16,1,128,128]{3,2,1,0:T(8,128)}, u32[]{:S(2)}) %copy-start.7) | copy-done | bytes 1048600
  28.8 0.7 copy-done.12
  29.5 0.7 copy-done.13
  30.2 42.0 %shard_map.114 = f32[16,4096]{1,0:T(8,128)S(1)} custom-call(f32[16,4096]{1,0:T(8,128)S(1)} %shard_map.113.source_ref, f32[128,128]{1,0:T(8,128)S(1)} %select_multiply_fusion.table_ref, f32[1,4096]{1,0:T(1,128)S(1)} %bitcast.2, f32[128,1]{1,0:T(8,128)S(1)} %multiply_multiply_fusion.shift_ref, s32[8,128]{1,0:T(8,128)S(1)} %copy-done.13, ...), custom_call_target="tpu_custom_call" | custom-call | tf_op jit(solution)/shard_map/pallas_call | solution.py:273
  72.2 1.3 %collective-permute-start.4 = (f32[16,128]{1,0:T(8,128)S(1)}, f32[16,128]{1,0:T(8,128)S(1)}, u32[]{:S(2)}, u32[]{:S(2)}) collective-permute-start(f32[16,128]{1,0:T(8,128)S(1)} %get-tuple-element.4), channel_id=1, source_target_pairs={{0,1},{2,3},{4,5},{6,7},{8,9},{10,11},{12,13},{14,15},{16,17},{18,... | collective-permute-start | bytes 24584 | tf_op jit(solution)/shard_map/ppermute | solution.py:23
  73.5 1.3 %collective-permute-start.5 = (f32[16,128]{1,0:T(8,128)S(1)}, f32[16,128]{1,0:T(8,128)S(1)}, u32[]{:S(2)}, u32[]{:S(2)}) collective-permute-start(f32[16,128]{1,0:T(8,128)S(1)} %get-tuple-element.5), channel_id=1, source_target_pairs={{1,0},{3,2},{5,4},{7,6},{9,8},{11,10},{13,12},{15,14},{17,16},{19,... | collective-permute-start | bytes 24584 | tf_op jit(solution)/shard_map/ppermute | solution.py:24
  74.8 0.8 collective-permute-start.6
  75.6 4.0 %collective-permute-start.7 = (f32[1,4096]{1,0:T(1,128)S(1)}, f32[1,4096]{1,0:T(1,128)S(1)}, u32[]{:S(2)}, u32[]{:S(2)}) collective-permute-start(f32[1,4096]{1,0:T(1,128)S(1)} %get-tuple-element.3), channel_id=1, source_target_pairs={{2,0},{4,2},{6,4},{8,6},{10,8},{12,10},{14,12},{0,14},{3,1},{5,3},... | collective-permute-start | bytes 49160 | tf_op jit(solution)/shard_map/ppermute | solution.py:24
  79.6 1.7 %collective-permute-done.6 = f32[1,4096]{1,0:T(1,128)S(1)} collective-permute-done((f32[1,4096]{1,0:T(1,128)S(1)}, f32[1,4096]{1,0:T(1,128)S(1)}, u32[]{:S(2)}, u32[]{:S(2)}) %collective-permute-start.6) | collective-permute-done | bytes 16416 | tf_op jit(solution)/shard_map/ppermute | solution.py:23
  81.4 6.4 %shard_map.115 = f32[16,4096]{1,0:T(8,128)} custom-call(s32[1]{0:T(128)} %bitcast.start_ref, f32[16,4352]{1,0:T(8,128)S(1)} %pad_maximum_fusion.1.wide_ref, f32[2,4096]{1,0:T(2,128)S(1)} %pad_maximum_fusion.3.edge_ref, f32[16,4096]{1,0:T(8,128)S(1)} %copy-done.2, f32[16,4096]{1,0:T(8,128)S(1)} %copy-done.5, f32[4,4096]{1,0:T(4,128)S(1)} %copy-done.9, ...), custom_call_target="tpu_custom_call" | custom-call | tf_op jit(solution)/shard_map/pallas_call | solution.py:101
  87.7 0.7 copy.15
  (31 shorter events, 0.2 us)
Async XLA Ops:
  1.3 10.9 %collective-permute-start = (f32[16,128]{1,0:T(8,128)S(1)}, f32[16,128]{1,0:T(8,128)S(1)}, u32[]{:S(2)}, u32[]{:S(2)}) collective-permute-start(f32[16,128]{1,0:T(8,128)S(1)} %get-tuple-element.8), channel_id=1, source_target_pairs={{0,1},{2,3},{4,5},{6,7},{8,9},{10,11},{12,13},{14,15},{16,17},{18,... | collective-permute-start | bytes 24584 | tf_op jit(solution)/shard_map/ppermute | solution.py:23
  3.7 8.6 %collective-permute-start.1 = (f32[16,128]{1,0:T(8,128)S(1)}, f32[16,128]{1,0:T(8,128)S(1)}, u32[]{:S(2)}, u32[]{:S(2)}) collective-permute-start(f32[16,128]{1,0:T(8,128)S(1)} %get-tuple-element.9), channel_id=1, source_target_pairs={{1,0},{3,2},{5,4},{7,6},{9,8},{11,10},{13,12},{15,14},{17,16},{19,... | collective-permute-start | bytes 24584 | tf_op jit(solution)/shard_map/ppermute | solution.py:24
  6.0 7.2 %collective-permute-start.2 = (f32[1,4096]{1,0:T(1,128)S(1)}, f32[1,4096]{1,0:T(1,128)S(1)}, u32[]{:S(2)}, u32[]{:S(2)}) collective-permute-start(f32[1,4096]{1,0:T(1,128)S(1)} %get-tuple-element.6), channel_id=1, source_target_pairs={{0,2},{2,4},{4,6},{6,8},{8,10},{10,12},{12,14},{14,0},{1,3},{3,5},... | collective-permute-start | bytes 49160 | tf_op jit(solution)/shard_map/ppermute | solution.py:23
  8.4 4.8 %collective-permute-start.3 = (f32[1,4096]{1,0:T(1,128)S(1)}, f32[1,4096]{1,0:T(1,128)S(1)}, u32[]{:S(2)}, u32[]{:S(2)}) collective-permute-start(f32[1,4096]{1,0:T(1,128)S(1)} %get-tuple-element.7), channel_id=1, source_target_pairs={{2,0},{4,2},{6,4},{8,6},{10,8},{12,10},{14,12},{0,14},{3,1},{5,3},... | collective-permute-start | bytes 49160 | tf_op jit(solution)/shard_map/ppermute | solution.py:24
  13.3 1.0 %copy-start.1 = (f32[16,4096]{1,0:T(8,128)S(1)}, f32[16,4096]{1,0:T(8,128)}, u32[]{:S(2)}) copy-start(f32[16,4096]{1,0:T(8,128)} %scalar_ref.3) | copy-start | bytes 786436
  14.3 0.9 %copy-start.4 = (f32[16,4096]{1,0:T(8,128)S(1)}, f32[16,4096]{1,0:T(8,128)}, u32[]{:S(2)}) copy-start(f32[16,4096]{1,0:T(8,128)} %vel_ref.3) | copy-start | bytes 786436
  15.2 0.8 copy-start.8
  16.0 0.8 copy-start.10
  22.5 2.2 %copy-start = (f32[16,4,128,128]{3,2,1,0:T(8,128)S(1)}, f32[16,4,128,128]{3,2,1,0:T(8,128)}, u32[]{:S(2)}) copy-start(f32[16,4,128,128]{3,2,1,0:T(8,128)} %one_hbm.1) | copy-start | bytes 12582916
  24.7 1.6 %copy-start.3 = (f32[16,2,128,128]{3,2,1,0:T(8,128)S(1)}, f32[16,2,128,128]{3,2,1,0:T(8,128)}, u32[]{:S(2)}) copy-start(f32[16,2,128,128]{3,2,1,0:T(8,128)} %two_hbm.1) | copy-start | bytes 6291460
  26.3 1.2 %copy-start.6 = (f32[16,1,128,128]{3,2,1,0:T(8,128)S(1)}, f32[16,1,128,128]{3,2,1,0:T(8,128)}, u32[]{:S(2)}) copy-start(f32[16,1,128,128]{3,2,1,0:T(8,128)} %three_hbm.1) | copy-start | bytes 3145732
  27.5 1.2 %copy-start.7 = (f32[16,1,128,128]{3,2,1,0:T(8,128)S(1)}, f32[16,1,128,128]{3,2,1,0:T(8,128)}, u32[]{:S(2)}) copy-start(f32[16,1,128,128]{3,2,1,0:T(8,128)} %root_hbm.1) | copy-start | bytes 3145732
  28.8 0.7 copy-start.12
  29.5 0.7 copy-start.13
  30.2 51.2 %copy-start.2 = (f32[16,4096]{1,0:T(8,128)S(1)}, f32[16,4096]{1,0:T(8,128)}, u32[]{:S(2)}) copy-start(f32[16,4096]{1,0:T(8,128)} %scalar_ref.3) | copy-start | bytes 786436
  30.2 51.2 %copy-start.5 = (f32[16,4096]{1,0:T(8,128)S(1)}, f32[16,4096]{1,0:T(8,128)}, u32[]{:S(2)}) copy-start(f32[16,4096]{1,0:T(8,128)} %vel_ref.3) | copy-start | bytes 786436
  30.2 51.2 %copy-start.9 = (f32[4,4096]{1,0:T(4,128)S(1)}, f32[4,4096]{1,0:T(4,128)}, u32[]{:S(2)}) copy-start(f32[4,4096]{1,0:T(4,128)} %weight_ref.3) | copy-start | bytes 196612
  30.2 51.2 %copy-start.11 = (s32[4,4096]{1,0:T(4,128)S(1)}, s32[4,4096]{1,0:T(4,128)}, u32[]{:S(2)}) copy-start(s32[4,4096]{1,0:T(4,128)} %near_ref.3) | copy-start | bytes 196612
  72.2 7.4 %collective-permute-start.4 = (f32[16,128]{1,0:T(8,128)S(1)}, f32[16,128]{1,0:T(8,128)S(1)}, u32[]{:S(2)}, u32[]{:S(2)}) collective-permute-start(f32[16,128]{1,0:T(8,128)S(1)} %get-tuple-element.4), channel_id=1, source_target_pairs={{0,1},{2,3},{4,5},{6,7},{8,9},{10,11},{12,13},{14,15},{16,17},{18,... | collective-permute-start | bytes 24584 | tf_op jit(solution)/shard_map/ppermute | solution.py:23
  73.5 6.1 %collective-permute-start.5 = (f32[16,128]{1,0:T(8,128)S(1)}, f32[16,128]{1,0:T(8,128)S(1)}, u32[]{:S(2)}, u32[]{:S(2)}) collective-permute-start(f32[16,128]{1,0:T(8,128)S(1)} %get-tuple-element.5), channel_id=1, source_target_pairs={{1,0},{3,2},{5,4},{7,6},{9,8},{11,10},{13,12},{15,14},{17,16},{19,... | collective-permute-start | bytes 24584 | tf_op jit(solution)/shard_map/ppermute | solution.py:24
  74.8 6.5 %collective-permute-start.6 = (f32[1,4096]{1,0:T(1,128)S(1)}, f32[1,4096]{1,0:T(1,128)S(1)}, u32[]{:S(2)}, u32[]{:S(2)}) collective-permute-start(f32[1,4096]{1,0:T(1,128)S(1)} %get-tuple-element.2), channel_id=1, source_target_pairs={{0,2},{2,4},{4,6},{6,8},{8,10},{10,12},{12,14},{14,0},{1,3},{3,5},... | collective-permute-start | bytes 49160 | tf_op jit(solution)/shard_map/ppermute | solution.py:23
  75.6 5.8 %collective-permute-start.7 = (f32[1,4096]{1,0:T(1,128)S(1)}, f32[1,4096]{1,0:T(1,128)S(1)}, u32[]{:S(2)}, u32[]{:S(2)}) collective-permute-start(f32[1,4096]{1,0:T(1,128)S(1)} %get-tuple-element.3), channel_id=1, source_target_pairs={{2,0},{4,2},{6,4},{8,6},{10,8},{12,10},{14,12},{0,14},{3,1},{5,3},... | collective-permute-start | bytes 49160 | tf_op jit(solution)/shard_map/ppermute | solution.py:24

commit v4 on v3

--- a/solution.py
+++ b/solution.py
@@ -11,19 +11,6 @@
 PLANES = 128
 CELL_DOM = 512
 HALO = 64
-
-
-def extended(value, sides, width, wrap):
-    for axis, dim in sides:
-        count, length = (lax.axis_size(axis), value.shape[dim])
-        up = [(i, (i + 1) % count) for i in range(count if wrap else count - 1)]
-        down = [(j, i) for i, j in up]
-        last = lax.slice_in_dim(value, length - width, length, axis=dim)
-        initial = lax.slice_in_dim(value, 0, width, axis=dim)
-        before = lax.ppermute(last, axis, up)
-        after = lax.ppermute(initial, axis, down)
-        value = jnp.concatenate([before, value, after], axis=dim)
-    return value
 
 
 def fourier_entry(wave_ids, plane_ids):
@@ -78,33 +65,17 @@
     return (ahead - behind)[:rows]
 
 
-def stencil_kernel(start_ref, wide_ref, edge_ref, scalar_ref, vel_ref, weight_ref, near_ref, out_ref):
-    start = start_ref[0]
-
+def stepped(start, wide, edge, scalar_ref, vel_ref, weight_ref, near_ref, out_ref):
     @pl.loop(0, out_ref.shape[1] // LANES)
     def _(block):
         at = pl.ds(pl.multiple_of(block * LANES, LANES), LANES)
         left, here, right = (
-            wide_ref[:, pl.ds(pl.multiple_of((block + i) * LANES, LANES), LANES)] for i in range(3)
+            wide[:, pl.ds(pl.multiple_of((block + i) * LANES, LANES), LANES)] for i in range(3)
         )
         near = near_ref[:, at] - (start + block * LANES - HALO)
         flux = flux_of(left, here, right, near, weight_ref[:, at])
-        change = plane_difference(here, edge_ref[0:1, at], edge_ref[1:2, at])
+        change = plane_difference(here, edge[0:1, at], edge[8:9, at])
         out_ref[:, at] = scalar_ref[:, at] - (vel_ref[:, at] * 0.5 * change + flux)
-
-
-def stepped(scalar, field, span_vel, flux_weight, neighbours, start):
-    planes_ext = extended(field, (("span", 0),), 1, True)
-    edge = jnp.concatenate([planes_ext[:1], planes_ext[-1:]], axis=0)
-    wide = extended(field, (("dom", 1),), LANES, False)
-    vmem = pl.BlockSpec(memory_space=pltpu.VMEM)
-    return pl.pallas_call(
-        stencil_kernel,
-        out_shape=jax.ShapeDtypeStruct(field.shape, field.dtype),
-        in_specs=[pl.BlockSpec(memory_space=pltpu.SMEM)] + [vmem] * 6,
-        out_specs=vmem,
-        compiler_params=pltpu.CompilerParams(vmem_limit_bytes=32 * 2**20),
-    )(start.reshape(1), wide, edge, scalar, span_vel, flux_weight, neighbours)
 
 
 def exact_dot(left, right, dims):
@@ -145,11 +116,12 @@
 
 
 def spectral_kernel(
-    span_count, source_ref, table_ref, diag_ref, shift_ref, iface_ref, one_hbm, two_hbm, three_hbm, root_hbm, out_ref,
+    span_count, scalar_ref, vel_ref, weight_ref, near_ref, table_ref, diag_ref, shift_ref, iface_ref,
+    one_hbm, two_hbm, three_hbm, root_hbm, out_ref, corrected_ref, source_ref, wide, later, edge, later_edge,
     one, two, three, root, source_in, leaf_out, leaf_in, press_out, press_in, back_in, fix_out, fix_in,
-    s0, s1, s2, s3, g0, g1, g2, g3, partner, load_sem, send_sem, recv_sem, swap_sem,
+    s0, s1, s2, s3, g0, g1, g2, g3, partner, load_sem, send_sem, recv_sem, swap_sem, halo_sem,
 ):
-    planes, cells = source_ref.shape
+    planes, cells = scalar_ref.shape
     cols = cells // span_count
     domains, slots = iface_ref.shape
     shares = span_count // domains
@@ -163,11 +135,42 @@
     ]
     for load in loads:
         load.start()
+    for field in (wide, later):
+        for place in (0, LANES + cells):
+            field[:, place : place + LANES] = jnp.zeros((planes, LANES), jnp.float32)
+    wide[:, LANES : LANES + cells] = scalar_ref[...]
     peers = [lax.rem(me + i, span_count) for i in range(1, span_count)]
     for peer in peers:
         pl.semaphore_signal(barrier, inc=1, device_id={"span": peer}, device_id_type=kind)
     pl.semaphore_signal(barrier, inc=1, device_id={"dom": 1 - half}, device_id_type=kind)
     pl.semaphore_wait(barrier, span_count)
+
+    def halo(phase, field, rows):
+        own = pl.ds(LANES, cells)
+        block_from = pl.ds(pl.multiple_of((1 - half) * (cells - LANES) + LANES, LANES), LANES)
+        block_to = pl.ds(pl.multiple_of(half * (cells + LANES), LANES), LANES)
+        plan = (
+            (field.at[pl.ds(planes - 1, 1), own], rows.at[pl.ds(0, 1)], {"span": lax.rem(me + 1, span_count)}),
+            (field.at[pl.ds(0, 1), own], rows.at[pl.ds(8, 1)], {"span": lax.rem(me + span_count - 1, span_count)}),
+            (field.at[:, block_from], field.at[:, block_to], {"dom": 1 - half}),
+        )
+        copies = [
+            pltpu.make_async_remote_copy(
+                src_ref=source,
+                dst_ref=target,
+                send_sem=halo_sem.at[phase, 0, i],
+                recv_sem=halo_sem.at[phase, 1, i],
+                device_id=device,
+                device_id_type=kind,
+            )
+            for i, (source, target, device) in enumerate(plan)
+        ]
+        for copy in copies:
+            copy.start()
+        for copy in copies:
+            copy.wait_send()
+        for copy in copies:
+            copy.wait_recv()
 
     def exchange(phase, pick, landing):
         copies = []
@@ -196,6 +199,9 @@
         cell = lax.broadcasted_iota(jnp.int32, (cols, slots), 0) + first
         return (cell == domain_row).astype(jnp.float32)
 
+    constants = (scalar_ref, vel_ref, weight_ref, near_ref)
+    halo(0, wide, edge)
+    stepped(half * cells, wide, edge, *constants, source_ref)
     sent = exchange(0, lambda peer: source_ref.at[:, columns_of(peer)], source_in)
     source_in[me] = source_ref[:, columns_of(me)]
     own_domain = lax.div(me, shares)
@@ -253,15 +259,20 @@
         domain = lax.div(owner, shares)
         where = hot(iface_ref[pl.ds(domain, 1), :], half * cells + owner * cols)
         added = exact_dot(fix_in[domain * shares], where, ((1,), (1,)))
-        out_ref[:, columns_of(owner)] = press_in[owner] - added
+        value = press_in[owner] - added
+        out_ref[:, columns_of(owner)] = value
+        later[:, pl.ds(pl.multiple_of(owner * cols + LANES, LANES), cols)] = value
+
+    halo(1, later, later_edge)
+    stepped(half * cells, later, later_edge, *constants, corrected_ref)
 
     for copies in (sent, leaves, pressed, backs, fixes, [swap]):
         for copy in copies:
             copy.wait_send()
 
 
-def projected(source, table, diagonal, shift, interface, blocks, span_count):
-    planes, cells = source.shape
+def projected(scalar, vel, weight, near, table, diagonal, shift, interface, blocks, span_count):
+    planes, cells = scalar.shape
     cols = cells // span_count
     domains, slots = interface.shape
     vmem = pl.BlockSpec(memory_space=pltpu.VMEM)
@@ -269,24 +280,27 @@
     wide, narrow = (span_count, planes, cols), (span_count, planes, slots)
     nodes = [domains >> level for level in range(4)]
     levels = [(node, planes, slots) for node in nodes]
+    fields = [(planes, cells)] + [(planes, cells + 2 * LANES)] * 2 + [(16, cells)] * 2
     shapes = [wide, narrow, narrow, wide, wide, narrow, narrow, narrow] + levels + levels + [levels[3]]
     return pl.pallas_call(
         functools.partial(spectral_kernel, span_count),
-        out_shape=jax.ShapeDtypeStruct(source.shape, source.dtype),
-        in_specs=[vmem] * 5 + [hbm] * 4,
-        out_specs=vmem,
-        scratch_shapes=[pltpu.VMEM(block.shape, block.dtype) for block in blocks]
+        out_shape=(jax.ShapeDtypeStruct(scalar.shape, scalar.dtype),) * 2,
+        in_specs=[vmem] * 8 + [hbm] * 4,
+        out_specs=(vmem, vmem),
+        scratch_shapes=[pltpu.VMEM(shape, jnp.float32) for shape in fields]
+        + [pltpu.VMEM(block.shape, block.dtype) for block in blocks]
         + [pltpu.VMEM(shape, jnp.float32) for shape in shapes]
         + [
             pltpu.SemaphoreType.DMA((4,)),
             pltpu.SemaphoreType.DMA((5, span_count - 1)),
             pltpu.SemaphoreType.DMA((5, span_count - 1)),
             pltpu.SemaphoreType.DMA((2,)),
+            pltpu.SemaphoreType.DMA((2, 2, 3)),
         ],
         compiler_params=pltpu.CompilerParams(
             collective_id=0, has_side_effects=True, vmem_limit_bytes=40 * 2**20
         ),
-    )(source, table, diagonal, shift, interface, *blocks)
+    )(scalar, vel, weight, near, table, diagonal, shift, interface, *blocks)
 
 
 def on_device(
@@ -301,17 +315,22 @@
     schur_three,
     schur_root,
 ):
-    cell_start = lax.axis_index("dom") * scalar.shape[1]
     waves = jnp.arange(PLANES, dtype=jnp.int32)
     table = fourier_entry(waves[:, None], waves[None, :])
     shift = wave_shift(waves)[:, None]
-    source = stepped(scalar, scalar, span_vel, flux_weight, neighbours, cell_start)
     blocks = (schur_one, schur_two, schur_three, schur_root)
-    pressure = projected(
-        source, table, diagonal[None, :], shift, interface, blocks, lax.axis_size("span")
-    )
-    corrected = stepped(scalar, pressure, span_vel, flux_weight, neighbours, cell_start)
-    return (pressure, corrected)
+    return projected(
+        scalar,
+        span_vel,
+        flux_weight,
+        neighbours,
+        table,
+        diagonal[None, :],
+        shift,
+        interface,
+        blocks,
+        lax.axis_size("span"),
+    )
 
 
 def solution(mesh):

time: 89.1 us -> 74.6 us (0.84)
  starting transfers between devices: 16.5 us -> 0 us
  Pallas kernels: 54 us -> 60.1 us
  waiting for transfers between devices: 1.72 us -> 0 us
  local copies, waits for them, and re-layouts: 13.8 us -> 12.7 us
  other arithmetic: 1.65 us -> 0.59 us
    pallas_call x1, Pallas kernels: 42 us -> 60.1 us  [projected(): pl.pallas_call(functools.partial(spectral_kernel, span_count), out_shape=...]
    ppermute x8 -> x0, starting transfers between devices: 16.5 us -> none  [the longest x4 9.71 us: extended(): after = lax.ppermute(initial, axis, down)]
    pallas_call x2 -> x0, Pallas kernels: 12 us -> none  [stepped(): pl.pallas_call(stencil_kernel, out_shape=jax.ShapeDtypeStruct(field.shape...]
    slice x4 -> x0, local copies, waits for them, and re-layouts: 1.74 us -> none  [extended(): last = lax.slice_in_dim(value, length - width, length, axis=dim)]
    ppermute x8 -> x0, waiting for transfers between devices: 1.72 us -> none  [the longest x4 1.71 us: extended(): before = lax.ppermute(last, axis, up)]
    concatenate x4 -> x0, other arithmetic: 1.06 us -> none  [the longest x2 0.99 us: extended(): value = jnp.concatenate([before, value, after], axis=dim)]
    unnamed x29 -> x22, local copies, waits for them, and re-layouts: 11.9 us -> 12.6 us
  transfers between devices with their start and end apart: 8 -> 0, of which waited for: 1 -> 0; matrix products, arithmetic and copies ran while one was open for 3% -> 0% of each run, Pallas kernels for 0% -> 0%
where the time goes in v4:
time: 74.6 us; the launch traced here: 74.1 us
  Pallas kernels  60.1 us (81%)
  local copies, waits for them, and re-layouts  12.7 us (17%)
    pallas_call x1, Pallas kernels, projected(): pl.pallas_call(functools.partial(spectral_kernel, span_count), out_shape=...  60.1 us
    unnamed x22, local copies, waits for them, and re-layouts  12.6 us

profile of v4, /device:TPU:0, one launch (start us, length us, event | category | flops | bytes accessed | tf_op | source)
XLA Modules:
  0.0 74.1 jit_solution(9965645699342457487)
XLA Ops:
  0.7 0.3 select_multiply_fusion.table_ref
  1.0 0.1 copy.13
  1.1 0.2 multiply_multiply_fusion.shift_ref
  1.4 0.0 copy-start
  1.4 2.2 %copy-done = f32[16,4,128,128]{3,2,1,0:T(8,128)S(1)} copy-done((f32[16,4,128,128]{3,2,1,0:T(8,128)S(1)}, f32[16,4,128,128]{3,2,1,0:T(8,128)}, u32[]{:S(2)}) %copy-start) | copy-done | bytes 4194328
  3.6 0.0 copy-start.1
  3.6 1.6 %copy-done.1 = f32[16,2,128,128]{3,2,1,0:T(8,128)S(1)} copy-done((f32[16,2,128,128]{3,2,1,0:T(8,128)S(1)}, f32[16,2,128,128]{3,2,1,0:T(8,128)}, u32[]{:S(2)}) %copy-start.1) | copy-done | bytes 2097176
  5.2 0.0 copy-start.2
  5.2 1.2 %copy-done.2 = f32[16,1,128,128]{3,2,1,0:T(8,128)S(1)} copy-done((f32[16,1,128,128]{3,2,1,0:T(8,128)S(1)}, f32[16,1,128,128]{3,2,1,0:T(8,128)}, u32[]{:S(2)}) %copy-start.2) | copy-done | bytes 1048600
  6.4 0.0 copy-start.3
  6.4 1.2 %copy-done.3 = f32[16,1,128,128]{3,2,1,0:T(8,128)S(1)} copy-done((f32[16,1,128,128]{3,2,1,0:T(8,128)S(1)}, f32[16,1,128,128]{3,2,1,0:T(8,128)}, u32[]{:S(2)}) %copy-start.3) | copy-done | bytes 1048600
  7.6 0.0 copy-start.4
  7.6 0.9 %copy-done.4 = f32[16,4096]{1,0:T(8,128)S(1)} copy-done((f32[16,4096]{1,0:T(8,128)S(1)}, f32[16,4096]{1,0:T(8,128)}, u32[]{:S(2)}) %copy-start.4) | copy-done | bytes 262168
  8.6 0.0 copy-start.5
  8.6 0.9 %copy-done.5 = f32[16,4096]{1,0:T(8,128)S(1)} copy-done((f32[16,4096]{1,0:T(8,128)S(1)}, f32[16,4096]{1,0:T(8,128)}, u32[]{:S(2)}) %copy-start.5) | copy-done | bytes 262168
  9.5 0.0 copy-start.6
  9.5 0.8 %copy-done.6 = f32[4,4096]{1,0:T(4,128)S(1)} copy-done((f32[4,4096]{1,0:T(4,128)S(1)}, f32[4,4096]{1,0:T(4,128)}, u32[]{:S(2)}) %copy-start.6) | copy-done | bytes 65560
  10.3 0.0 copy-start.7
  10.3 0.8 %copy-done.7 = s32[4,4096]{1,0:T(4,128)S(1)} copy-done((s32[4,4096]{1,0:T(4,128)S(1)}, s32[4,4096]{1,0:T(4,128)}, u32[]{:S(2)}) %copy-start.7) | copy-done | bytes 65560
  11.2 0.0 copy-start.8
  11.2 0.7 copy-done.8
  11.9 0.0 copy-start.9
  11.9 0.7 copy-done.9
  12.6 60.1 %shard_map.113 = (f32[16,4096]{1,0:T(8,128)S(1)}, f32[16,4096]{1,0:T(8,128)S(1)}) custom-call(f32[16,4096]{1,0:T(8,128)S(1)} %copy-done.4, f32[16,4096]{1,0:T(8,128)S(1)} %copy-done.5, f32[4,4096]{1,0:T(4,128)S(1)} %copy-done.6, s32[4,4096]{1,0:T(4,128)S(1)} %copy-done.7, f32[128,128]{1,0:T(8,128)S(1)} %select_multiply_fusion.table_ref, ...), custom_call_target="tpu_custom_call" | custom-call | tf_op jit(solution)/shard_map/pallas_call | solution.py:285
  72.7 0.7 copy.16
  73.4 0.7 copy.17
  (4 shorter events, 0.0 us)
Async XLA Ops:
  1.4 2.2 %copy-start = (f32[16,4,128,128]{3,2,1,0:T(8,128)S(1)}, f32[16,4,128,128]{3,2,1,0:T(8,128)}, u32[]{:S(2)}) copy-start(f32[16,4,128,128]{3,2,1,0:T(8,128)} %one_hbm.1) | copy-start | bytes 12582916
  3.6 1.6 %copy-start.1 = (f32[16,2,128,128]{3,2,1,0:T(8,128)S(1)}, f32[16,2,128,128]{3,2,1,0:T(8,128)}, u32[]{:S(2)}) copy-start(f32[16,2,128,128]{3,2,1,0:T(8,128)} %two_hbm.1) | copy-start | bytes 6291460
  5.2 1.2 %copy-start.2 = (f32[16,1,128,128]{3,2,1,0:T(8,128)S(1)}, f32[16,1,128,128]{3,2,1,0:T(8,128)}, u32[]{:S(2)}) copy-start(f32[16,1,128,128]{3,2,1,0:T(8,128)} %three_hbm.1) | copy-start | bytes 3145732
  6.4 1.2 %copy-start.3 = (f32[16,1,128,128]{3,2,1,0:T(8,128)S(1)}, f32[16,1,128,128]{3,2,1,0:T(8,128)}, u32[]{:S(2)}) copy-start(f32[16,1,128,128]{3,2,1,0:T(8,128)} %root_hbm.1) | copy-start | bytes 3145732
  7.6 0.9 %copy-start.4 = (f32[16,4096]{1,0:T(8,128)S(1)}, f32[16,4096]{1,0:T(8,128)}, u32[]{:S(2)}) copy-start(f32[16,4096]{1,0:T(8,128)} %scalar_ref.1) | copy-start | bytes 786436
  8.6 0.9 %copy-start.5 = (f32[16,4096]{1,0:T(8,128)S(1)}, f32[16,4096]{1,0:T(8,128)}, u32[]{:S(2)}) copy-start(f32[16,4096]{1,0:T(8,128)} %vel_ref.1) | copy-start | bytes 786436
  9.5 0.8 %copy-start.6 = (f32[4,4096]{1,0:T(4,128)S(1)}, f32[4,4096]{1,0:T(4,128)}, u32[]{:S(2)}) copy-start(f32[4,4096]{1,0:T(4,128)} %weight_ref.1) | copy-start | bytes 196612
  10.3 0.8 %copy-start.7 = (s32[4,4096]{1,0:T(4,128)S(1)}, s32[4,4096]{1,0:T(4,128)}, u32[]{:S(2)}) copy-start(s32[4,4096]{1,0:T(4,128)} %near_ref.1) | copy-start | bytes 196612
  11.2 0.7 copy-start.8
  11.9 0.7 copy-start.9

commit v5 on v4

--- a/solution.py
+++ b/solution.py
@@ -66,7 +66,7 @@
 
 
 def stepped(start, wide, edge, scalar_ref, vel_ref, weight_ref, near_ref, out_ref):
-    @pl.loop(0, out_ref.shape[1] // LANES)
+    @pl.loop(0, out_ref.shape[1] // LANES, unroll=4)
     def _(block):
         at = pl.ds(pl.multiple_of(block * LANES, LANES), LANES)
         left, here, right = (

time: 74.6 us -> 67.6 us (0.906)
  Pallas kernels: 60.1 us -> 53.1 us
    pallas_call x1, Pallas kernels: 60.1 us -> 53.1 us  [projected(): pl.pallas_call(functools.partial(spectral_kernel, span_count), out_shape=...]
where the time goes in v5:
time: 67.6 us; the launch traced here: 67.1 us
  Pallas kernels  53.1 us (79%)
  local copies, waits for them, and re-layouts  12.7 us (19%)
  between operations  0.69 us (1%)
    pallas_call x1, Pallas kernels, projected(): pl.pallas_call(functools.partial(spectral_kernel, span_count), out_shape=...  53.1 us
    unnamed x22, local copies, waits for them, and re-layouts  12.6 us

profile of v5, /device:TPU:0, one launch (start us, length us, event | category | flops | bytes accessed | tf_op | source)
XLA Modules:
  0.0 67.1 jit_solution(17949129294376364937)
XLA Ops:
  0.7 0.3 select_multiply_fusion.table_ref
  1.0 0.1 copy.13
  1.1 0.2 multiply_multiply_fusion.shift_ref
  1.4 0.0 copy-start
  1.4 2.2 %copy-done = f32[16,4,128,128]{3,2,1,0:T(8,128)S(1)} copy-done((f32[16,4,128,128]{3,2,1,0:T(8,128)S(1)}, f32[16,4,128,128]{3,2,1,0:T(8,128)}, u32[]{:S(2)}) %copy-start) | copy-done | bytes 4194328
  3.6 0.0 copy-start.1
  3.6 1.6 %copy-done.1 = f32[16,2,128,128]{3,2,1,0:T(8,128)S(1)} copy-done((f32[16,2,128,128]{3,2,1,0:T(8,128)S(1)}, f32[16,2,128,128]{3,2,1,0:T(8,128)}, u32[]{:S(2)}) %copy-start.1) | copy-done | bytes 2097176
  5.2 0.0 copy-start.2
  5.2 1.2 %copy-done.2 = f32[16,1,128,128]{3,2,1,0:T(8,128)S(1)} copy-done((f32[16,1,128,128]{3,2,1,0:T(8,128)S(1)}, f32[16,1,128,128]{3,2,1,0:T(8,128)}, u32[]{:S(2)}) %copy-start.2) | copy-done | bytes 1048600
  6.4 0.0 copy-start.3
  6.4 1.2 %copy-done.3 = f32[16,1,128,128]{3,2,1,0:T(8,128)S(1)} copy-done((f32[16,1,128,128]{3,2,1,0:T(8,128)S(1)}, f32[16,1,128,128]{3,2,1,0:T(8,128)}, u32[]{:S(2)}) %copy-start.3) | copy-done | bytes 1048600
  7.6 0.0 copy-start.4
  7.6 0.9 %copy-done.4 = f32[16,4096]{1,0:T(8,128)S(1)} copy-done((f32[16,4096]{1,0:T(8,128)S(1)}, f32[16,4096]{1,0:T(8,128)}, u32[]{:S(2)}) %copy-start.4) | copy-done | bytes 262168
  8.6 0.0 copy-start.5
  8.6 0.9 %copy-done.5 = f32[16,4096]{1,0:T(8,128)S(1)} copy-done((f32[16,4096]{1,0:T(8,128)S(1)}, f32[16,4096]{1,0:T(8,128)}, u32[]{:S(2)}) %copy-start.5) | copy-done | bytes 262168
  9.5 0.0 copy-start.6
  9.5 0.8 %copy-done.6 = f32[4,4096]{1,0:T(4,128)S(1)} copy-done((f32[4,4096]{1,0:T(4,128)S(1)}, f32[4,4096]{1,0:T(4,128)}, u32[]{:S(2)}) %copy-start.6) | copy-done | bytes 65560
  10.3 0.0 copy-start.7
  10.3 0.8 %copy-done.7 = s32[4,4096]{1,0:T(4,128)S(1)} copy-done((s32[4,4096]{1,0:T(4,128)S(1)}, s32[4,4096]{1,0:T(4,128)}, u32[]{:S(2)}) %copy-start.7) | copy-done | bytes 65560
  11.2 0.0 copy-start.8
  11.2 0.7 %copy-done.8 = f32[4096]{0:T(1024)S(1)} copy-done((f32[4096]{0:T(1024)S(1)}, f32[4096]{0:T(1024)}, u32[]{:S(2)}) %copy-start.8) | copy-done | bytes 16408
  11.9 0.0 copy-start.9
  11.9 0.7 %copy-done.9 = s32[8,128]{1,0:T(8,128)S(1)} copy-done((s32[8,128]{1,0:T(8,128)S(1)}, s32[8,128]{1,0:T(8,128)}, u32[]{:S(2)}) %copy-start.9) | copy-done | bytes 4120
  12.6 53.1 %shard_map.113 = (f32[16,4096]{1,0:T(8,128)S(1)}, f32[16,4096]{1,0:T(8,128)S(1)}) custom-call(f32[16,4096]{1,0:T(8,128)S(1)} %copy-done.4, f32[16,4096]{1,0:T(8,128)S(1)} %copy-done.5, f32[4,4096]{1,0:T(4,128)S(1)} %copy-done.6, s32[4,4096]{1,0:T(4,128)S(1)} %copy-done.7, f32[128,128]{1,0:T(8,128)S(1)} %select_multiply_fusion.table_ref, ...), custom_call_target="tpu_custom_call" | custom-call | tf_op jit(solution)/shard_map/pallas_call | solution.py:285
  65.7 0.7 %copy.16 = f32[16,4096]{1,0:T(8,128)} copy(f32[16,4096]{1,0:T(8,128)S(1)} %get-tuple-element.4) | data formatting | bytes 524288
  66.4 0.7 %copy.17 = f32[16,4096]{1,0:T(8,128)} copy(f32[16,4096]{1,0:T(8,128)S(1)} %get-tuple-element.5) | data formatting | bytes 524288
  (4 shorter events, 0.0 us)
Async XLA Ops:
  1.4 2.2 %copy-start = (f32[16,4,128,128]{3,2,1,0:T(8,128)S(1)}, f32[16,4,128,128]{3,2,1,0:T(8,128)}, u32[]{:S(2)}) copy-start(f32[16,4,128,128]{3,2,1,0:T(8,128)} %one_hbm.1) | copy-start | bytes 12582916
  3.6 1.6 %copy-start.1 = (f32[16,2,128,128]{3,2,1,0:T(8,128)S(1)}, f32[16,2,128,128]{3,2,1,0:T(8,128)}, u32[]{:S(2)}) copy-start(f32[16,2,128,128]{3,2,1,0:T(8,128)} %two_hbm.1) | copy-start | bytes 6291460
  5.2 1.2 %copy-start.2 = (f32[16,1,128,128]{3,2,1,0:T(8,128)S(1)}, f32[16,1,128,128]{3,2,1,0:T(8,128)}, u32[]{:S(2)}) copy-start(f32[16,1,128,128]{3,2,1,0:T(8,128)} %three_hbm.1) | copy-start | bytes 3145732
  6.4 1.2 %copy-start.3 = (f32[16,1,128,128]{3,2,1,0:T(8,128)S(1)}, f32[16,1,128,128]{3,2,1,0:T(8,128)}, u32[]{:S(2)}) copy-start(f32[16,1,128,128]{3,2,1,0:T(8,128)} %root_hbm.1) | copy-start | bytes 3145732
  7.6 0.9 %copy-start.4 = (f32[16,4096]{1,0:T(8,128)S(1)}, f32[16,4096]{1,0:T(8,128)}, u32[]{:S(2)}) copy-start(f32[16,4096]{1,0:T(8,128)} %scalar_ref.1) | copy-start | bytes 786436
  8.6 0.9 %copy-start.5 = (f32[16,4096]{1,0:T(8,128)S(1)}, f32[16,4096]{1,0:T(8,128)}, u32[]{:S(2)}) copy-start(f32[16,4096]{1,0:T(8,128)} %vel_ref.1) | copy-start | bytes 786436
  9.5 0.8 %copy-start.6 = (f32[4,4096]{1,0:T(4,128)S(1)}, f32[4,4096]{1,0:T(4,128)}, u32[]{:S(2)}) copy-start(f32[4,4096]{1,0:T(4,128)} %weight_ref.1) | copy-start | bytes 196612
  10.3 0.8 %copy-start.7 = (s32[4,4096]{1,0:T(4,128)S(1)}, s32[4,4096]{1,0:T(4,128)}, u32[]{:S(2)}) copy-start(s32[4,4096]{1,0:T(4,128)} %near_ref.1) | copy-start | bytes 196612
  11.2 0.7 %copy-start.8 = (f32[4096]{0:T(1024)S(1)}, f32[4096]{0:T(1024)}, u32[]{:S(2)}) copy-start(f32[4096]{0:T(1024)} %param.14) | copy-start | bytes 49156
  11.9 0.7 %copy-start.9 = (s32[8,128]{1,0:T(8,128)S(1)}, s32[8,128]{1,0:T(8,128)}, u32[]{:S(2)}) copy-start(s32[8,128]{1,0:T(8,128)} %iface_ref.1) | copy-start | bytes 12292
